TPU v7x, 32 devices: a whole 2x2x4 slice. The times are simulated.
32 devices in a mesh: dp: 8 (over z, x), head: 4 (over y, core).
Axes of the slice: x: 2, y: 2, z: 4, core: 2. Of those that a mesh axis runs over, the one named last changes fastest.
Arguments:
- tokens: bfloat16 [32768, 512], P(('dp', 'head')), may hold values from -6 to 6
- doc_ids: int32 [16, 2048], P('dp'), may hold values from 0 to 15, never falling along the last dimension, each value on 1 to 1024 neighbouring positions
- pad_mask: int32 [16, 2048], P('dp'), may hold values 0 or 1
- norm1_gain: bfloat16 [512], replicated, may hold values from 0.5 to 1.5
- norm1_shift: bfloat16 [512], replicated, may hold values from -4 to 4
- w_qkv: bfloat16 [3, 512, 512], P(None, None, 'head'), may hold values from -0.25 to 0.25
- w_out: bfloat16 [512, 512], P('head'), may hold values from -2 to 2
- norm2_gain: bfloat16 [512], replicated, may hold values from 0.5 to 1.5
- norm2_shift: bfloat16 [512], replicated, may hold values from -4 to 4
- w_hidden: bfloat16 [512, 2048], P(None, 'head'), may hold values from -0.25 to 0.25
- hidden_bias: bfloat16 [2048], P('head'), may hold values from -4 to 4
- w_return: bfloat16 [2048, 512], P('head'), may hold values from -0.25 to 0.25
- return_bias: bfloat16 [512], replicated, may hold values from -4 to 4
- out_grad: bfloat16 [32768, 512], P(('dp', 'head')), may hold values from -6 to 6
Outputs:
- output: bfloat16 [32768, 512], P(('dp', 'head'))
- tokens_grad: float32 [32768, 512], P(('dp', 'head'))
- norm1_gain_grad: float32 [512], replicated
- norm1_shift_grad: float32 [512], replicated
- w_qkv_grad: float32 [3, 512, 512], P(None, None, 'head')
- w_out_grad: float32 [512, 512], P('head')
- norm2_gain_grad: float32 [512], replicated
- norm2_shift_grad: float32 [512], replicated
- w_hidden_grad: float32 [512, 2048], P(None, 'head')
- hidden_bias_grad: float32 [2048], P('head')
- w_return_grad: float32 [2048, 512], P('head')
- return_bias_grad: float32 [512], replicated
Inputs may be any that keep to these rules, and one draw needn't show every extreme that they name: `doc_ids`: along each row the document numbers never fall; each number from 0 up covers 1 to 1024 consecutive positions of the row.
All inputs are finite; a program needn't handle non-finite values. No bound on the sum of `pad_mask` on one device may be relied on, other than what follows from the above.
Results may differ from a plain program's by a relative error of at most 0.012.
Values may be sent and summed in bfloat16 or wider, within the bound.
No kernel may reach another device: no remote copies, remote signals or barrier semaphores. Data moves between devices by JAX's collectives and lax.ppermute only.
A program may use at most 192 MiB of HBM per device.

v0:
```python
import jax
import jax.numpy as jnp
from jax import lax
from jax.sharding import PartitionSpec as P

HEAD_DIM = 64
LEN = 2048
SPAN = 512


epsilon = 1e-05


def layer_norm(values, norm_gain, norm_shift):
    centre = values - jnp.mean(values, axis=-1, keepdims=True)
    spread = jnp.mean(centre * centre, axis=-1, keepdims=True)
    return centre * lax.rsqrt(spread + epsilon) * norm_gain + norm_shift


def feature(values):
    return jax.nn.elu(values) + 1.0


def smooth(values):
    return jax.nn.gelu(values, approximate=False)


def span_view(values, row_count, head_count):
    return jnp.swapaxes(values.reshape(row_count, -1, SPAN, head_count, HEAD_DIM), 0, 1)


def span_flat(values):
    swapped = jnp.swapaxes(values, 0, 1)
    return swapped.reshape(
        swapped.shape[0] * swapped.shape[1] * swapped.shape[2], swapped.shape[3] * swapped.shape[4]
    )


def block_flags(segment, previous):
    reads_state = (segment == previous[:, None]).astype(jnp.float32)
    in_last = (segment == segment[:, -1:]).astype(jnp.bfloat16)
    carried = (segment[:, -1] == previous).astype(jnp.float32)
    return (reads_state, in_last, carried)


def span_masks(segment, previous):
    length = segment.shape[1]
    causal = lax.broadcasted_iota(jnp.int32, (length, length), 0) >= lax.broadcasted_iota(
        jnp.int32, (length, length), 1
    )
    allowed = ((segment[:, :, None] == segment[:, None, :]) & causal[None]).astype(jnp.float32)
    reads_state, in_last, carried = block_flags(segment, previous)
    return (allowed, reads_state, in_last, carried)


def forward_step(running, pieces):
    memory, key_total = running
    queries, keys_feat, values, segment, previous = pieces
    allowed, reads_state, in_last, carried = span_masks(segment, previous)
    scores = (
        jnp.einsum("rthe,rshe->rhts", queries, keys_feat, preferred_element_type=jnp.float32)
        * allowed[:, None]
    )
    weighted = jnp.einsum(
        "rhts,rshf->rthf", scores.astype(jnp.bfloat16), values, preferred_element_type=jnp.float32
    )
    weighted = weighted + reads_state[:, :, None, None] * jnp.einsum(
        "rthe,rhef->rthf", queries, memory.astype(jnp.bfloat16), preferred_element_type=jnp.float32
    )
    totals = jnp.swapaxes(jnp.sum(scores, axis=-1), 1, 2) + reads_state[:, :, None] * jnp.sum(
        queries.astype(jnp.float32) * key_total[:, None], axis=-1
    )
    chosen = keys_feat * in_last[:, :, None, None]
    increment = jnp.einsum("rshe,rshf->rhef", chosen, values, preferred_element_type=jnp.float32)
    new_memory = carried[:, None, None, None] * memory + increment
    new_total = carried[:, None, None] * key_total + jnp.sum(chosen.astype(jnp.float32), axis=1)
    return ((new_memory, new_total), (memory, key_total, weighted, totals))


def backward_step(running, pieces):
    memory_grad, total_grad = running
    queries, keys_feat, values, segment, previous, memory, key_total, weighted_grad, totals_grad = (
        pieces
    )
    allowed, reads_state, in_last, carried = span_masks(segment, previous)
    scores = (
        jnp.einsum("rthe,rshe->rhts", queries, keys_feat, preferred_element_type=jnp.float32)
        * allowed[:, None]
    )
    score_grad = (
        jnp.einsum("rthf,rshf->rhts", weighted_grad, values, preferred_element_type=jnp.float32)
        + jnp.swapaxes(totals_grad, 1, 2)[..., None]
    )
    score_grad = (score_grad * allowed[:, None]).astype(jnp.bfloat16)
    state_term = (
        jnp.einsum(
            "rthf,rhef->rthe",
            weighted_grad,
            memory.astype(jnp.bfloat16),
            preferred_element_type=jnp.float32,
        )
        + totals_grad[..., None] * key_total[:, None]
    )
    queries_grad = (
        jnp.einsum("rhts,rshe->rthe", score_grad, keys_feat, preferred_element_type=jnp.float32)
        + reads_state[:, :, None, None] * state_term
    )
    increment_grad = memory_grad.astype(jnp.bfloat16)
    last_weight = in_last.astype(jnp.float32)[:, :, None, None]
    keys_grad = jnp.einsum(
        "rhts,rthe->rshe", score_grad, queries, preferred_element_type=jnp.float32
    )
    keys_grad = keys_grad + last_weight * (
        jnp.einsum("rshf,rhef->rshe", values, increment_grad, preferred_element_type=jnp.float32)
        + total_grad[:, None]
    )
    chosen = keys_feat * in_last[:, :, None, None]
    values_grad = jnp.einsum(
        "rhts,rthf->rshf",
        scores.astype(jnp.bfloat16),
        weighted_grad,
        preferred_element_type=jnp.float32,
    )
    values_grad = values_grad + jnp.einsum(
        "rshe,rhef->rshf", chosen, increment_grad, preferred_element_type=jnp.float32
    )
    reading = queries * reads_state.astype(jnp.bfloat16)[:, :, None, None]
    new_memory_grad = carried[:, None, None, None] * memory_grad + jnp.einsum(
        "rthe,rthf->rhef", reading, weighted_grad, preferred_element_type=jnp.float32
    )
    new_total_grad = carried[:, None, None] * total_grad + jnp.sum(
        reading.astype(jnp.float32) * totals_grad[..., None], axis=1
    )
    return ((new_memory_grad, new_total_grad), (queries_grad, keys_grad, values_grad))


def body(
    tokens,
    doc_ids,
    pad_mask,
    norm1_gain,
    norm1_shift,
    w_qkv,
    w_out,
    norm2_gain,
    norm2_shift,
    w_hidden,
    hidden_bias,
    w_return,
    return_bias,
    out_grad,
):
    rows_here = doc_ids.shape[0]
    inputs = tokens.astype(jnp.float32)
    normed1, norm1_back = jax.vjp(
        layer_norm, inputs, norm1_gain.astype(jnp.float32), norm1_shift.astype(jnp.float32)
    )
    normed1_low = normed1.astype(jnp.bfloat16)
    heads_here = w_qkv.shape[2] // HEAD_DIM
    spans = LEN // SPAN
    normed1_all = lax.all_gather(normed1_low, "head", axis=0, tiled=True)
    projected = jnp.einsum("td,pde->pte", normed1_all, w_qkv, preferred_element_type=jnp.float32)
    live = pad_mask.reshape(-1).astype(jnp.float32)[:, None]
    query_feat, query_back = jax.vjp(feature, projected[0])
    key_feat, key_back = jax.vjp(feature, projected[1])
    queries = span_view(query_feat.astype(jnp.bfloat16), rows_here, heads_here)
    keys_low = span_view((key_feat * live).astype(jnp.bfloat16), rows_here, heads_here)
    values = span_view(projected[2].astype(jnp.bfloat16), rows_here, heads_here)
    doc_blocks = jnp.swapaxes(doc_ids.reshape(rows_here, spans, SPAN), 0, 1)
    previous = jnp.concatenate(
        [jnp.full((1, rows_here), -1, jnp.int32), doc_blocks[:-1, :, -1]], axis=0
    )
    live_blocks = jnp.swapaxes(pad_mask.reshape(rows_here, spans, SPAN), 0, 1).astype(jnp.float32)[
        ..., None, None
    ]
    start = (
        jnp.zeros((rows_here, heads_here, HEAD_DIM, HEAD_DIM), jnp.float32),
        jnp.zeros((rows_here, heads_here, HEAD_DIM), jnp.float32),
    )
    ignored, (memories, key_totals, weighted, totals) = lax.scan(
        forward_step, start, (queries, keys_low, values, doc_blocks, previous)
    )
    bounded = jnp.maximum(totals, 1.0)
    mixed = span_flat(weighted / bounded[..., None] * live_blocks).astype(jnp.bfloat16)
    attended = lax.psum_scatter(
        jnp.dot(mixed, w_out, preferred_element_type=jnp.float32),
        "head",
        scatter_dimension=0,
        tiled=True,
    )
    residual = inputs + attended
    normed2, norm2_back = jax.vjp(
        layer_norm, residual, norm2_gain.astype(jnp.float32), norm2_shift.astype(jnp.float32)
    )
    normed2_low = normed2.astype(jnp.bfloat16)
    grad_out = out_grad.astype(jnp.float32)
    return_bias_grad = jnp.sum(grad_out, axis=0)
    normed2_all = lax.all_gather(normed2_low, "head", axis=0, tiled=True)
    hidden_pre = jnp.dot(
        normed2_all, w_hidden, preferred_element_type=jnp.float32
    ) + hidden_bias.astype(jnp.float32)
    activated, smooth_back = jax.vjp(smooth, hidden_pre)
    activated_low = activated.astype(jnp.bfloat16)
    branch = lax.psum_scatter(
        jnp.dot(activated_low, w_return, preferred_element_type=jnp.float32).astype(jnp.bfloat16),
        "head",
        scatter_dimension=0,
        tiled=True,
    ).astype(jnp.float32)
    output = (residual + branch + return_bias.astype(jnp.float32)).astype(jnp.bfloat16)
    grad_all = lax.all_gather(out_grad, "head", axis=0, tiled=True)
    w_return_grad = jnp.einsum(
        "tf,td->fd", activated_low, grad_all, preferred_element_type=jnp.float32
    )
    activated_grad = jnp.einsum("td,fd->tf", grad_all, w_return, preferred_element_type=jnp.float32)
    hidden_grad = smooth_back(activated_grad)[0].astype(jnp.bfloat16)
    hidden_bias_grad = jnp.sum(hidden_grad.astype(jnp.float32), axis=0)
    w_hidden_grad = jnp.einsum(
        "td,tf->df", normed2_all, hidden_grad, preferred_element_type=jnp.float32
    )
    normed2_grad = lax.psum_scatter(
        jnp.einsum("tf,df->td", hidden_grad, w_hidden, preferred_element_type=jnp.float32),
        "head",
        scatter_dimension=0,
        tiled=True,
    )
    residual_part, norm2_gain_grad, norm2_shift_grad = norm2_back(normed2_grad)
    residual_grad = grad_out + residual_part
    residual_low = residual_grad.astype(jnp.bfloat16)
    residual_all = lax.all_gather(residual_low, "head", axis=0, tiled=True)
    w_out_grad = jnp.einsum("te,td->ed", mixed, residual_all, preferred_element_type=jnp.float32)
    mixed_grad = (
        span_view(
            jnp.einsum("td,ed->te", residual_all, w_out, preferred_element_type=jnp.float32),
            rows_here,
            heads_here,
        )
        * live_blocks
    )
    weighted_grad = (mixed_grad / bounded[..., None]).astype(jnp.bfloat16)
    totals_grad = (
        -jnp.sum(mixed_grad * weighted, axis=-1)
        / (bounded * bounded)
        * (totals > 1.0).astype(jnp.float32)
    )
    ignored, (queries_grad, keys_grad, values_grad) = lax.scan(
        backward_step,
        start,
        (
            queries,
            keys_low,
            values,
            doc_blocks,
            previous,
            memories,
            key_totals,
            weighted_grad,
            totals_grad,
        ),
        reverse=True,
    )
    query_pre_grad = query_back(span_flat(queries_grad))[0].astype(jnp.bfloat16)
    key_pre_grad = key_back(span_flat(keys_grad) * live)[0].astype(jnp.bfloat16)
    value_pre_grad = span_flat(values_grad).astype(jnp.bfloat16)
    projected_grad = jnp.stack([query_pre_grad, key_pre_grad, value_pre_grad])
    w_qkv_grad = jnp.einsum(
        "td,pte->pde", normed1_all, projected_grad, preferred_element_type=jnp.float32
    )
    normed1_grad = lax.psum_scatter(
        jnp.einsum("pte,pde->td", projected_grad, w_qkv, preferred_element_type=jnp.float32).astype(
            jnp.bfloat16
        ),
        "head",
        scatter_dimension=0,
        tiled=True,
    ).astype(jnp.float32)
    inputs_part, norm1_gain_grad, norm1_shift_grad = norm1_back(normed1_grad)
    tokens_grad = residual_grad + inputs_part
    w_qkv_grad, w_out_grad, w_hidden_grad, hidden_bias_grad, w_return_grad = lax.psum(
        (w_qkv_grad, w_out_grad, w_hidden_grad, hidden_bias_grad, w_return_grad), "dp"
    )
    norm1_gain_grad, norm1_shift_grad, norm2_gain_grad, norm2_shift_grad, return_bias_grad = (
        lax.psum(
            (
                norm1_gain_grad,
                norm1_shift_grad,
                norm2_gain_grad,
                norm2_shift_grad,
                return_bias_grad,
            ),
            ("dp", "head"),
        )
    )
    return (
        output,
        tokens_grad,
        norm1_gain_grad,
        norm1_shift_grad,
        w_qkv_grad,
        w_out_grad,
        norm2_gain_grad,
        norm2_shift_grad,
        w_hidden_grad,
        hidden_bias_grad,
        w_return_grad,
        return_bias_grad,
    )


def solution(mesh):
    return jax.shard_map(
        body,
        mesh=mesh,
        in_specs=(
            P(("dp", "head"), None),
            P("dp", None),
            P("dp", None),
            P(),
            P(),
            P(None, None, "head"),
            P("head", None),
            P(),
            P(),
            P(None, "head"),
            P("head"),
            P("head", None),
            P(),
            P(("dp", "head"), None),
        ),
        out_specs=(
            P(("dp", "head"), None),
            P(("dp", "head"), None),
            P(),
            P(),
            P(None, None, "head"),
            P("head", None),
            P(),
            P(),
            P(None, "head"),
            P("head"),
            P("head", None),
            P(),
        ),
        check_vma=False,
    )
```

profile of v0, /device:TPU:0, one launch (start us, length us, event | category | flops | bytes accessed | tf_op | source)
XLA Modules:
  0.0 892.1 jit_solution(1975763088832320398)
XLA Ops:
  14.4 35.6 %all-gather.5.cloned.1.call-done = bf16[4096,512]{1,0:T(8,128)(2,1)} async-done(((bf16[1024,512]{1,0:T(8,128)(2,1)}), bf16[4096,512]{1,0:T(8,128)(2,1)}) %all-gather.5.cloned.1.call-update) | async-done | bytes 4194320 | tf_op jit(solution)/shard_map/all_gather | solution.py:161
  50.0 4.5 convolution_bitcast_fusion.4
  54.6 2.4 fusion.132
  61.7 2.4 squeeze.96
  64.1 3.5 fusion.119
  70.8 2.4 squeeze.97
  73.2 3.4 fusion.118
  80.6 96.1 %while.46 = (s32[]{:T(128)}, f32[2,2,64,64]{3,2,1,0:T(8,128)S(1)}, f32[2,2,64]{2,1,0:T(2,128)S(1)}, bf16[4,2,2,64,64]{4,3,2,1,0:T(8,128)(2,1)S(1)}, f32[4,2,2,64...) while((s32[]{:T(128)}, f32[2,2,64,64]{3,2,1,0:T(8,128)S(1)}, ...), condition=%wide.region_6.7_spmd.clone.clone, body=%wide.region_2.6_spmd.clone.sunk.clone | while | flops 309285376 | bytes 25746696 | solution.py:180
  81.8 3.8 multiply_reduce_fusion.14
  86.8 2.9 fusion.223
  90.2 11.0 %dynamic_update_slice.71 = f32[4,2,512,2,64]{2,0,1,4,3:T(4,128)} dynamic-update-slice(f32[4,2,512,2,64]{2,0,1,4,3:T(4,128)} %get-tuple-element.1061, f32[1,2,512,2,64]{2,0,1,4,3:T(1,128)S(1)} %copy.250, s32[]{:T(128)} %get-tuple-element.1056, s32[]{:T(128)} %constant.147.clone.1..sunk.2, s32[]{:T(128)} %constant.147.clone.1..sunk.2, s32[]{:T(128)} %constant.147.clone.1..sunk.2, ...) | dynamic-update-slice | bytes 1048580 | tf_op jit(solution)/shard_map/while/body/jit(dynamic_update_index_in_dim)/dynamic_update_slice | solution.py:180
  105.8 3.8 multiply_reduce_fusion.14
  110.8 2.9 fusion.223
  114.2 11.0 %dynamic_update_slice.71 = f32[4,2,512,2,64]{2,0,1,4,3:T(4,128)} dynamic-update-slice(f32[4,2,512,2,64]{2,0,1,4,3:T(4,128)} %get-tuple-element.1061, f32[1,2,512,2,64]{2,0,1,4,3:T(1,128)S(1)} %copy.250, s32[]{:T(128)} %get-tuple-element.1056, s32[]{:T(128)} %constant.147.clone.1..sunk.2, s32[]{:T(128)} %constant.147.clone.1..sunk.2, s32[]{:T(128)} %constant.147.clone.1..sunk.2, ...) | dynamic-update-slice | bytes 1048580 | tf_op jit(solution)/shard_map/while/body/jit(dynamic_update_index_in_dim)/dynamic_update_slice | solution.py:180
  129.8 3.8 multiply_reduce_fusion.14
  134.8 2.9 fusion.223
  138.3 11.0 %dynamic_update_slice.71 = f32[4,2,512,2,64]{2,0,1,4,3:T(4,128)} dynamic-update-slice(f32[4,2,512,2,64]{2,0,1,4,3:T(4,128)} %get-tuple-element.1061, f32[1,2,512,2,64]{2,0,1,4,3:T(1,128)S(1)} %copy.250, s32[]{:T(128)} %get-tuple-element.1056, s32[]{:T(128)} %constant.147.clone.1..sunk.2, s32[]{:T(128)} %constant.147.clone.1..sunk.2, s32[]{:T(128)} %constant.147.clone.1..sunk.2, ...) | dynamic-update-slice | bytes 1048580 | tf_op jit(solution)/shard_map/while/body/jit(dynamic_update_index_in_dim)/dynamic_update_slice | solution.py:180
  153.8 3.8 multiply_reduce_fusion.14
  158.8 2.9 fusion.223
  162.3 11.0 %dynamic_update_slice.71 = f32[4,2,512,2,64]{2,0,1,4,3:T(4,128)} dynamic-update-slice(f32[4,2,512,2,64]{2,0,1,4,3:T(4,128)} %get-tuple-element.1061, f32[1,2,512,2,64]{2,0,1,4,3:T(1,128)S(1)} %copy.250, s32[]{:T(128)} %get-tuple-element.1056, s32[]{:T(128)} %constant.147.clone.1..sunk.2, s32[]{:T(128)} %constant.147.clone.1..sunk.2, s32[]{:T(128)} %constant.147.clone.1..sunk.2, ...) | dynamic-update-slice | bytes 1048580 | tf_op jit(solution)/shard_map/while/body/jit(dynamic_update_index_in_dim)/dynamic_update_slice | solution.py:180
  180.5 4.6 fusion.133
  186.9 70.1 %reduce-scatter.5.cloned.1.call-done = f32[1024,512]{1,0:T(8,128)} async-done(((f32[4096,512]{1,0:T(8,128)}), f32[1024,512]{1,0:T(8,128)}) %reduce-scatter.5.cloned.1.call-update) | async-done | bytes 2097168 | tf_op jit(solution)/shard_map/reduce_scatter | solution.py:185
  264.0 32.8 %all-gather.7.cloned.1.call-done = bf16[4096,512]{1,0:T(8,128)(2,1)} async-done(((bf16[1024,512]{1,0:T(8,128)(2,1)}), bf16[4096,512]{1,0:T(8,128)(2,1)}) %all-gather.7.cloned.1.call-update) | async-done | bytes 4194320 | tf_op jit(solution)/shard_map/all_gather | solution.py:198
  296.8 7.8 fusion.134
  304.5 28.2 %all-gather.9.cloned.1.call-done = bf16[4096,512]{1,0:T(8,128)(2,1)} async-done(((bf16[1024,512]{1,0:T(8,128)(2,1)}), bf16[4096,512]{1,0:T(8,128)(2,1)}) %all-gather.9.cloned.1.call-update) | async-done | bytes 4194320 | tf_op jit(solution)/shard_map/all_gather | solution.py:211
  332.8 25.4 %convert_reduce_fusion.1 = (f32[512]{0:T(512)}, bf16[4096,512]{1,0:T(8,128)(2,1)S(1)}, f32[4096,512]{1,0:T(8,128)}) fusion(f32[4096,512]{1,0:T(8,128)} %fusion.134, f32[512]{0:T(512)} %convert_element_type.335, bf16[4096,512]{1,0:T(8,128)(2,1)} %all-gather.9.cloned.1.call-done, bf16[512,512]{1,0:T(8,128)(2,1)S(1)} %copy-done), kind=kOutput, calls=%fused_computation.131 | convolution fusion | flops 2304769536 | bytes 25694208 | tf_op jit(solution)/shard_map/td,fd->tf/dot_general | solution.py:215
  360.2 5.8 fusion.135
  366.7 11.2 %multiply_convert_fusion.10 = bf16[4096,512]{1,0:T(8,128)(2,1)} fusion(f32[4096,512]{1,0:T(8,128)} %get-tuple-element.745, f32[4096,512]{1,0:T(8,128)} %fusion.134, f32[512]{0:T(512)S(1)} %copy-done.56), kind=kLoop, calls=%fused_computation.133 | loop fusion | flops 8388608 | bytes 20973568 | tf_op jit(solution)/shard_map/convert_element_type | solution.py:203
  377.9 7.5 convolution_convert_fusion
  386.1 51.8 %reduce-scatter.9.cloned.1.call-done = f32[1024,512]{1,0:T(8,128)} async-done(((f32[4096,512]{1,0:T(8,128)}), f32[1024,512]{1,0:T(8,128)}) %reduce-scatter.9.cloned.1.call-update) | async-done | bytes 2097168 | tf_op jit(solution)/shard_map/reduce_scatter | solution.py:221
  437.9 2.4 multiply_reduce_fusion.3
  440.4 44.5 %reduce-scatter.7.cloned.1.call-done = bf16[1024,512]{1,0:T(8,128)(2,1)} async-done(((bf16[4096,512]{1,0:T(8,128)(2,1)}), bf16[1024,512]{1,0:T(8,128)(2,1)}) %reduce-scatter.7.cloned.1.call-update) | async-done | bytes 1048592 | tf_op jit(solution)/shard_map/reduce_scatter | solution.py:204
  484.9 3.4 fusion.130
  492.2 6.9 fusion.138
  499.1 3.3 fusion.139
  502.5 23.1 %all-gather.11.cloned.1.call-done = bf16[4096,512]{1,0:T(8,128)(2,1)} async-done(((bf16[1024,512]{1,0:T(8,128)(2,1)}), bf16[4096,512]{1,0:T(8,128)(2,1)}) %all-gather.11.cloned.1.call-update) | async-done | bytes 4194320 | tf_op jit(solution)/shard_map/all_gather | solution.py:230
  525.6 3.7 fusion.136
  529.3 2.6 reshape.448
  531.9 3.3 multiply_reduce_fusion.4
  539.7 74.1 %while.47 = (s32[]{:T(128)}, f32[2,2,64,64]{3,2,1,0:T(8,128)S(1)}, f32[2,2,64]{2,1,0:T(2,128)S(1)}, f32[4,2,512,2,64]{2,4,3,1,0:T(8,128)}, f32[4,2,512,2,64]{2,4...) while((s32[]{:T(128)}, f32[2,2,64,64]{3,2,1,0:T(8,128)S(1)}, ...), condition=%wide.region_17.18_spmd.clone.clone, body=%wide.region_15.17_spmd.clone.sunk.clone | while | flops 747198976 | bytes 38523748 | solution.py:246
  549.8 2.5 fusion.241
  552.3 3.0 fusion.244
  568.3 2.5 fusion.241
  570.8 3.0 fusion.244
  586.8 2.5 fusion.241
  589.3 3.0 fusion.244
  605.4 2.5 fusion.241
  607.9 3.0 fusion.244
  613.8 6.7 copy.213
  620.5 4.3 reshape.453
  624.8 6.7 copy.215
  631.6 5.4 reshape.455
  637.0 6.0 copy.214
  643.0 4.7 reshape.454
  647.7 3.9 add_convert_fusion.2
  655.4 2.7 fusion.115
  659.4 5.6 bitcast_convert_fusion
  665.7 23.0 %psum.77 = f32[512]{0:T(512)} all-reduce(f32[512]{0:T(512)S(1)} %copy-done.57), channel_id=1, replica_groups=mesh['dp'=8,'head'=4] {'dp'}, use_global_device_ids=true, to_apply=%region_33.34 | all-reduce | flops 512 | bytes 4096 | tf_op jit(solution)/shard_map/psum | solution.py:279
  688.7 100.3 %all-reduce.5.cloned.1.call-done = (f32[3,512,128]{1,2,0:T(8,128)}, f32[128,512]{1,0:T(8,128)}, f32[512,512]{1,0:T(8,128)}, f32[512,512]{1,0:T(8,128)}) async-done(((f32[3,512,128]{1,2,0:T(8,128)}, f32[128,512]{1,0:T(8,128)}, f32[512,512]{1,0:T(8,128)}, f32[512,512]{1,0:T(8,128)}), (f32[3,512,128]{1,2,0:T(8,128)}, f32[128,512]{1,0:T(8,128)}, f32[512,512]{1,0:T(8,128)}, ...) | async-done | bytes 3145744 | tf_op jit(solution)/shard_map/psum | solution.py:279
  789.0 2.3 copy.207
  791.3 43.7 %reduce-scatter.11.cloned.1.call-done = bf16[1024,512]{1,0:T(8,128)(2,1)} async-done(((bf16[4096,512]{1,0:T(8,128)(2,1)}), bf16[1024,512]{1,0:T(8,128)(2,1)}) %reduce-scatter.11.cloned.1.call-update) | async-done | bytes 1048592 | tf_op jit(solution)/shard_map/reduce_scatter | solution.py:269
  837.3 2.4 fusion.105
  842.0 39.5 %all-reduce.1 = (f32[512]{0:T(512)}, f32[512]{0:T(512)}, f32[512]{0:T(512)}, f32[512]{0:T(512)}, f32[512]{0:T(512)}) all-reduce(f32[512]{0:T(512)S(1)} %get-tuple-element.663, f32[512]{0:T(512)S(1)} %get-tuple-element.666, f32[512]{0:T(512)S(1)} %get-tuple-element.661, ...), channel_id=1, replica_groups=mesh['dp'=8,'head'=4] {'dp','head'}, use_global_device_ids=true, to_apply=%region_22.23 | all-reduce | flops 2560 | bytes 20480 | tf_op jit(solution)/shard_map/psum | solution.py:283
  882.1 2.3 copy.306
  (361 shorter events, 131.7 us)
Async XLA Ops:
  7.2 325.6 %copy-start = (bf16[512,512]{1,0:T(8,128)(2,1)S(1)}, bf16[512,512]{1,0:T(8,128)(2,1)}, u32[]{:S(2)}) copy-start(bf16[512,512]{1,0:T(8,128)(2,1)} %param.29) | copy-start | bytes 1572868
  7.2 4.1 copy-start.4
  7.2 4.0 copy-start.58
  7.2 4.0 copy-start.59
  7.2 42.8 %all-gather.5.cloned.1.call-start = ((), (), s32[]{:S(2)}) async-start(), calls=%async_computation.4 | async-start | bytes 5242880 | tf_op jit(solution)/shard_map/all_gather | solution.py:161
  8.8 3.9 copy-start.34
  8.8 4.0 copy-start.54
  8.8 41.2 %copy-start.28 = (bf16[3,512,128]{2,1,0:T(8,128)(2,1)S(1)}, bf16[3,512,128]{2,1,0:T(8,128)(2,1)}, u32[]{:S(2)}) copy-start(bf16[3,512,128]{2,1,0:T(8,128)(2,1)} %param.23) | copy-start | bytes 1179652
  11.2 43.4 %copy-start.40 = (f32[1024]{0:T(1024)}, f32[1024]{0:T(1024)S(1)}, u32[]{:S(2)}) copy-start(f32[1024]{0:T(1024)S(1)} %fusion.122) | copy-start | bytes 12292
  11.2 43.4 %copy-start.45 = (f32[512]{0:T(512)}, f32[512]{0:T(512)S(1)}, u32[]{:S(2)}) copy-start(f32[512]{0:T(512)S(1)} %convert_element_type.320) | copy-start | bytes 6148
  12.7 244.2 %reduce-scatter.5.cloned.1.call-start = ((), (), s32[]{:S(2)}) async-start(), calls=%async_computation.5 | async-start | bytes 10485760 | tf_op jit(solution)/shard_map/reduce_scatter | solution.py:185
  54.6 3.9 copy-start.3
  73.2 4.7 copy-start.20
  89.6 12.4 %copy-start.2 = (bf16[4,2,512,2,64]{2,4,3,1,0:T(8,128)(2,1)S(1)}, bf16[4,2,512,2,64]{2,4,3,1,0:T(8,128)(2,1)}, u32[]{:S(2)}) copy-start(bf16[4,2,512,2,64]{2,4,3,1,0:T(8,128)(2,1)} %get-tuple-element.1077) | copy-start | bytes 3145732 | tf_op jit(solution)/shard_map/while
  113.7 12.4 %copy-start.2 = (bf16[4,2,512,2,64]{2,4,3,1,0:T(8,128)(2,1)S(1)}, bf16[4,2,512,2,64]{2,4,3,1,0:T(8,128)(2,1)}, u32[]{:S(2)}) copy-start(bf16[4,2,512,2,64]{2,4,3,1,0:T(8,128)(2,1)} %get-tuple-element.1077) | copy-start | bytes 3145732 | tf_op jit(solution)/shard_map/while
  137.7 12.4 %copy-start.2 = (bf16[4,2,512,2,64]{2,4,3,1,0:T(8,128)(2,1)S(1)}, bf16[4,2,512,2,64]{2,4,3,1,0:T(8,128)(2,1)}, u32[]{:S(2)}) copy-start(bf16[4,2,512,2,64]{2,4,3,1,0:T(8,128)(2,1)} %get-tuple-element.1077) | copy-start | bytes 3145732 | tf_op jit(solution)/shard_map/while
  161.7 12.4 %copy-start.2 = (bf16[4,2,512,2,64]{2,4,3,1,0:T(8,128)(2,1)S(1)}, bf16[4,2,512,2,64]{2,4,3,1,0:T(8,128)(2,1)}, u32[]{:S(2)}) copy-start(bf16[4,2,512,2,64]{2,4,3,1,0:T(8,128)(2,1)} %get-tuple-element.1077) | copy-start | bytes 3145732 | tf_op jit(solution)/shard_map/while
  176.7 3.8 copy-start.30
  177.3 3.2 copy-start.27
  180.5 4.6 copy-start.12
  185.1 111.7 %all-gather.7.cloned.1.call-start = ((), (), s32[]{:S(2)}) async-start(), calls=%async_computation.6 | async-start | bytes 5242880 | tf_op jit(solution)/shard_map/all_gather | solution.py:198
  259.1 1.7 copy-start.51
  260.7 36.0 %copy-start.21 = (bf16[512,512]{1,0:T(8,128)(2,1)S(1)}, bf16[512,512]{1,0:T(8,128)(2,1)}, u32[]{:S(2)}) copy-start(bf16[512,512]{1,0:T(8,128)(2,1)} %param.27) | copy-start | bytes 1572868
  262.1 70.6 %all-gather.9.cloned.1.call-start = ((), (), s32[]{:S(2)}) async-start(), calls=%async_computation.8 | async-start | bytes 5242880 | tf_op jit(solution)/shard_map/all_gather | solution.py:211
  262.7 175.2 %reduce-scatter.9.cloned.1.call-start = ((), (), s32[]{:S(2)}) async-start(), calls=%async_computation.9 | async-start | bytes 10485760 | tf_op jit(solution)/shard_map/reduce_scatter | solution.py:221
  358.1 2.1 copy-start.6
  366.1 118.8 %reduce-scatter.7.cloned.1.call-start = ((), (), s32[]{:S(2)}) async-start(), calls=%async_computation.7 | async-start | bytes 5242880 | tf_op jit(solution)/shard_map/reduce_scatter | solution.py:204
  385.4 52.5 %copy-start.39 = (f32[1024]{0:T(1024)S(1)}, f32[1024]{0:T(1024)}, u32[]{:S(2)}) copy-start(f32[1024]{0:T(1024)} %copy-done.38) | copy-start | bytes 12292
  385.4 52.5 %copy-start.44 = (f32[1024]{0:T(1024)S(1)}, f32[1024]{0:T(1024)}, u32[]{:S(2)}) copy-start(f32[1024]{0:T(1024)} %copy-done.43) | copy-start | bytes 12292
  385.4 52.5 %copy-start.52 = (f32[512]{0:T(512)S(1)}, f32[512]{0:T(512)}, u32[]{:S(2)}) copy-start(f32[512]{0:T(512)} %convert_element_type.332) | copy-start | bytes 6148
  385.5 140.1 %all-gather.11.cloned.1.call-start = ((), (), s32[]{:S(2)}) async-start(), calls=%async_computation.10 | async-start | bytes 5242880 | tf_op jit(solution)/shard_map/all_gather | solution.py:230
  386.1 54.2 %copy-start.50 = (f32[1024]{0:T(1024)S(1)}, f32[1024]{0:T(1024)}, u32[]{:S(2)}) copy-start(f32[1024]{0:T(1024)} %copy-done.49) | copy-start | bytes 12292
  484.9 4.8 copy-start.15
  490.9 298.1 %all-reduce.5.cloned.1.call-start = ((), (), s32[]{:S(2)}) async-start(), calls=%async_computation.12 | async-start | bytes 6291456 | tf_op jit(solution)/shard_map/psum | solution.py:279
  492.2 6.9 copy-start.7
  492.2 7.0 copy-start.11
  529.3 2.6 copy-start.31
  531.9 3.3 copy-start.37
  536.5 3.2 copy-start.33
  540.2 2.2 copy-start.1
  552.3 3.0 copy-start.18
  556.6 1.6 copy-start.19
  558.7 2.3 copy-start.1
  570.8 3.0 copy-start.18
  575.0 1.6 copy-start.19
  577.2 2.3 copy-start.1
  589.3 3.0 copy-start.18
  595.7 2.3 copy-start.1
  607.9 3.0 copy-start.18
  647.7 4.1 copy-start.8
  647.7 4.4 copy-start.13
  652.1 3.0 copy-start.14
  652.1 3.3 copy-start.22
  658.1 176.9 %reduce-scatter.11.cloned.1.call-start = ((), (), s32[]{:S(2)}) async-start(), calls=%async_computation.11 | async-start | bytes 5242880 | tf_op jit(solution)/shard_map/reduce_scatter | solution.py:269
  665.0 170.0 %copy-start.5 = (bf16[1024,512]{1,0:T(8,128)(2,1)S(1)}, bf16[1024,512]{1,0:T(8,128)(2,1)}, u32[]{:S(2)}) copy-start(bf16[1024,512]{1,0:T(8,128)(2,1)} %param.18) | copy-start | bytes 3145732
  665.0 170.0 %copy-start.35 = (f32[1024]{0:T(1024)S(1)}, f32[1024]{0:T(1024)}, u32[]{:S(2)}) copy-start(f32[1024]{0:T(1024)} %copy-done.34) | copy-start | bytes 12292
  665.0 170.0 %copy-start.46 = (f32[512]{0:T(512)S(1)}, f32[512]{0:T(512)}, u32[]{:S(2)}) copy-start(f32[512]{0:T(512)} %copy-done.45) | copy-start | bytes 6148
  665.1 172.2 %copy-start.48 = (f32[1024]{0:T(1024)S(1)}, f32[1024]{0:T(1024)}, u32[]{:S(2)}) copy-start(f32[1024]{0:T(1024)} %copy-done.47) | copy-start | bytes 12292
  665.1 172.2 %copy-start.41 = (f32[1024]{0:T(1024)S(1)}, f32[1024]{0:T(1024)}, u32[]{:S(2)}) copy-start(f32[1024]{0:T(1024)} %copy-done.40) | copy-start | bytes 12292
  791.3 48.4 %copy-start.16 = (bf16[1024,512]{1,0:T(8,128)(2,1)S(1)}, bf16[1024,512]{1,0:T(8,128)(2,1)}, u32[]{:S(2)}) copy-start(bf16[1024,512]{1,0:T(8,128)(2,1)} %param.31) | copy-start | bytes 3145732
  835.0 4.7 copy-start.10
  835.0 4.7 copy-start.17
  839.8 41.7 %copy-start.32 = (f32[128,512]{1,0:T(8,128)S(1)}, f32[128,512]{1,0:T(8,128)}, u32[]{:S(2)}) copy-start(f32[128,512]{1,0:T(8,128)} %get-tuple-element.1130) | copy-start | bytes 786436
  842.0 42.4 %copy-start.26 = (f32[512,512]{1,0:T(8,128)S(1)}, f32[512,512]{1,0:T(8,128)}, u32[]{:S(2)}) copy-start(f32[512,512]{1,0:T(8,128)} %get-tuple-element.1135) | copy-start | bytes 3145732
  (20 other events, 21.1 us)
Sparse Core Ops, SparseCore 0:
  12.8 37.1 all-gather.4
  185.2 71.7 reduce-scatter.4
  262.2 34.4 all-gather.6
  298.3 34.4 all-gather.8
  366.2 71.6 reduce-scatter.8
  440.3 44.5 reduce-scatter.6
  491.1 34.4 all-gather.10
  658.2 130.7 all-reduce.4
  791.5 43.4 reduce-scatter.10
where the time goes:
time: 900 us; the launch traced here: 892 us
  waiting for transfers between devices  431 us (48%)
  matrix products  176 us (20%)
  local copies, waits for them, and re-layouts  130 us (14%)
  other arithmetic  76.3 us (8%)
  blocking collectives  62.5 us (7%)
  between operations  14.7 us (2%)
    psum x1, waiting for transfers between devices, body(): lax.psum((w_qkv_grad, w_out_grad, w_hidden_grad, hidden_bias_grad, w_retu...  100 us
    reduce_scatter x1, waiting for transfers between devices, body(): lax.psum_scatter(jnp.dot(mixed, w_out, preferred_element_type=jnp.float32...  70.1 us
    reduce_scatter x1, waiting for transfers between devices, body(): lax.psum_scatter(jnp.einsum('tf,df->td', hidden_grad, w_hidden, preferred...  51.8 us
    dynamic_update_slice x16, local copies, waits for them, and re-layouts, body(): lax.scan(forward_step, start, (queries, keys_low, values, doc_blocks, pre...  46.4 us
    reduce_scatter x1, waiting for transfers between devices, body(): lax.psum_scatter(jnp.dot(activated_low, w_return, preferred_element_type=...  44.5 us
    reduce_scatter x1, waiting for transfers between devices, body(): lax.psum_scatter(jnp.einsum('pte,pde->td', projected_grad, w_qkv, preferr...  43.7 us
    psum x1, blocking collectives, body(): lax.psum((norm1_gain_grad, norm1_shift_grad, norm2_gain_grad, norm2_shift...  39.5 us
    all_gather x1, waiting for transfers between devices, body(): normed1_all = lax.all_gather(normed1_low, 'head', axis=0, tiled=True)  35.6 us
  transfers between devices with their start and end apart: 9, of which 9 were waited for; matrix products, arithmetic and copies ran while one was open for 6% of the time, Pallas kernels for 0%

commit v1 on v0

v1 whole, which is shorter than its diff:
```python
import functools

import jax
import jax.numpy as jnp
from jax import lax
from jax.experimental import pallas as pl
from jax.experimental.pallas import tpu as pltpu
from jax.sharding import PartitionSpec as P

HEAD_DIM = 64
PAIR = 2 * HEAD_DIM
CHUNK = 256
EPSILON = 1e-05
F32 = jnp.float32
BF16 = jnp.bfloat16
VMEM_BYTES = 60 * 1024 * 1024

DOC, LIVE, READ_HALF, READ_CHUNK, IN_LAST, CARRIED, FIRST_HALF = range(7)


def nn(a, b):
    return lax.dot_general(a, b, (((1,), (0,)), ((), ())), preferred_element_type=F32)


def nt(a, b):
    return lax.dot_general(a, b, (((1,), (1,)), ((), ())), preferred_element_type=F32)


def tn(a, b):
    return lax.dot_general(a, b, (((0,), (0,)), ((), ())), preferred_element_type=F32)


def normalise(x):
    centre = x - jnp.mean(x, axis=-1, keepdims=True)
    rstd = lax.rsqrt(jnp.mean(centre * centre, axis=-1, keepdims=True) + EPSILON)
    return centre * rstd, rstd


def head_lanes(shape):
    return lax.broadcasted_iota(jnp.int32, shape, len(shape) - 1) % PAIR < HEAD_DIM


def pair_mask(width):
    rows = lax.broadcasted_iota(jnp.int32, (PAIR, width), 0) < HEAD_DIM
    return rows == head_lanes((PAIR, width))


def allowed_mask(doc_col, doc_row):
    t = lax.broadcasted_iota(jnp.int32, (CHUNK, CHUNK), 0)
    s = lax.broadcasted_iota(jnp.int32, (CHUNK, CHUNK), 1)
    return (doc_col == doc_row) & (s <= t)


def feature(x):
    return jnp.where(x > 0, x + 1.0, jnp.exp(jnp.minimum(x, 0.0)))


def attend_kernel(blocks, first, *refs):
    refs = list(refs)
    take = refs.pop
    src = take(0)
    if first:
        gain, shift = take(0), take(0)
    w = [take(0) for _ in range(blocks)]
    cols, doc_row = take(0), take(0)
    if first:
        n1_out = take(0)
    q_out, k_out, v_out, num_out, tot_out, state_out, last_out, w_all, state = refs
    step = pl.program_id(0)

    @pl.when(step == 0)
    def _():
        for p in range(3):
            for b in range(blocks):
                w_all[p, :, b * PAIR : (b + 1) * PAIR] = w[b][p]
        state[...] = jnp.zeros_like(state)

    if first:
        xhat, _ = normalise(src[...].astype(F32))
        n1 = (xhat * gain[...].astype(F32) + shift[...].astype(F32)).astype(BF16)
        n1_out[...] = n1
    else:
        n1 = src[...]
    live = cols[:, LIVE : LIVE + 1]
    reads = cols[:, READ_CHUNK : READ_CHUNK + 1]
    in_last = cols[:, IN_LAST : IN_LAST + 1].astype(BF16)
    carried = cols[0:1, CARRIED : CARRIED + 1]
    mask = allowed_mask(cols[:, DOC : DOC + 1], doc_row[...])
    q_all = feature(nn(n1, w_all[0])).astype(BF16)
    k_all = (feature(nn(n1, w_all[1])) * live).astype(BF16)
    v_all = nn(n1, w_all[2]).astype(BF16)
    here = head_lanes((CHUNK, PAIR))
    block_diagonal = pair_mask(2 * PAIR)
    ones = jnp.ones((CHUNK, PAIR), BF16)
    zeros = jnp.zeros((CHUNK, PAIR), BF16)
    for b in range(blocks):
        lanes = slice(b * PAIR, (b + 1) * PAIR)
        q, k, v = q_all[:, lanes], k_all[:, lanes], v_all[:, lanes]
        q_out[b], k_out[b], v_out[b] = q, k, v
        total = jnp.zeros((CHUNK, 2 * PAIR), F32)
        for own in (here, jnp.logical_not(here)):
            scores = nt(jnp.where(own, q, zeros), k)
            scores = jnp.where(mask, scores, 0.0).astype(BF16)
            wide = jnp.concatenate([jnp.where(own, v, zeros), jnp.where(own, ones, zeros)], axis=1)
            total = total + nn(scores, wide)
        low = state[b].astype(BF16)
        state_out[0, b] = low
        total = total + reads * nn(q, low)
        num_out[b] = total[:, :PAIR]
        tot_out[b] = total[:, PAIR:]
        grown = tn(k * in_last, jnp.concatenate([v, ones], axis=1))
        state[b] = carried * state[b] + jnp.where(block_diagonal, grown, 0.0)
        last_out[b ^ 1] = state[b].astype(BF16)


def attend(src, norm, w, cols, doc_row):
    tokens, width = src.shape
    blocks, chunks = len(w), tokens // CHUNK
    first = norm is not None
    whole = lambda shape: pl.BlockSpec(shape, lambda i: (0,) * len(shape))
    rows = lambda n: pl.BlockSpec((CHUNK, n), lambda i: (i, 0))
    part = lambda: pl.BlockSpec((blocks, CHUNK, PAIR), lambda i: (0, i, 0))
    in_specs = [rows(width)] + ([whole((1, width))] * 2 if first else [])
    in_specs += [whole((3, width, PAIR))] * blocks
    in_specs += [rows(8), pl.BlockSpec((1, CHUNK), lambda i: (0, i))]
    arrays = [src] + (list(norm) if first else []) + list(w) + [cols, doc_row]
    out_shape = [jax.ShapeDtypeStruct((tokens, width), BF16)] if first else []
    out_specs = [rows(width)] if first else []
    out_shape += [jax.ShapeDtypeStruct((blocks, tokens, PAIR), BF16)] * 3
    out_shape += [jax.ShapeDtypeStruct((blocks, tokens, PAIR), F32)] * 2
    out_shape += [jax.ShapeDtypeStruct((chunks, blocks, PAIR, 2 * PAIR), BF16)]
    out_shape += [jax.ShapeDtypeStruct((blocks, PAIR, 2 * PAIR), BF16)]
    out_specs += [part()] * 5
    out_specs += [pl.BlockSpec((1, blocks, PAIR, 2 * PAIR), lambda i: (i, 0, 0, 0))]
    out_specs += [whole((blocks, PAIR, 2 * PAIR))]
    return pl.pallas_call(
        functools.partial(attend_kernel, blocks, first),
        grid=(chunks,),
        in_specs=in_specs,
        out_specs=out_specs,
        out_shape=out_shape,
        scratch_shapes=[
            pltpu.VMEM((3, width, blocks * PAIR), BF16),
            pltpu.VMEM((blocks, PAIR, 2 * PAIR), F32),
        ],
        compiler_params=pltpu.CompilerParams(
            dimension_semantics=("arbitrary",), vmem_limit_bytes=VMEM_BYTES
        ),
        cost_estimate=pl.CostEstimate(
            flops=2 * tokens * blocks * PAIR * (3 * width + 4 * CHUNK),
            bytes_accessed=8 << 20,
            transcendentals=0,
        ),
        name="attend",
    )(*arrays)


def mix_kernel(groups, tok, *refs):
    refs = list(refs)
    q = [refs.pop(0) for _ in range(groups)]
    num = [refs.pop(0) for _ in range(groups)]
    tot = [refs.pop(0) for _ in range(groups)]
    come = [refs.pop(0) for _ in range(groups)]
    wo = [refs.pop(0) for _ in range(2 * groups)]
    cols, gain, shift, mixed_out, inv_out, residual_out, n2_out, w_all = refs

    @pl.when(pl.program_id(0) == 0)
    def _():
        for b in range(2 * groups):
            w_all[b * PAIR : (b + 1) * PAIR, :] = wo[b][:PAIR, :]

    live = cols[:, LIVE : LIVE + 1]
    reads = cols[:, READ_HALF : READ_HALF + 1]
    for b in range(2 * groups):
        g, i = divmod(b, 2)
        lanes = slice(b * PAIR, (b + 1) * PAIR)
        far = reads * nn(q[g][i], come[g][i])
        inv = 1.0 / jnp.maximum(tot[g][i] + far[:, PAIR:], 1.0)
        inv_out[:, lanes] = inv
        mixed_out[:, lanes] = ((num[g][i] + far[:, :PAIR]) * inv * live).astype(BF16)
    residual = tok[...].astype(F32) + nn(mixed_out[...], w_all[...])
    residual_out[...] = residual
    xhat, _ = normalise(residual)
    n2_out[...] = (xhat * gain[...].astype(F32) + shift[...].astype(F32)).astype(BF16)


def mix(tok, q, num, tot, come, wo, cols, gain, shift):
    tokens, width = tok.shape
    groups = len(q)
    whole = lambda shape: pl.BlockSpec(shape, lambda i: (0,) * len(shape))
    rows = lambda n: pl.BlockSpec((CHUNK, n), lambda i: (i, 0))
    part = pl.BlockSpec((2, CHUNK, PAIR), lambda i: (0, i, 0))
    return pl.pallas_call(
        functools.partial(mix_kernel, groups),
        grid=(tokens // CHUNK,),
        in_specs=[rows(width)]
        + [part] * (3 * groups)
        + [whole((2, PAIR, 2 * PAIR))] * groups
        + [whole(wo[0].shape)] * (2 * groups)
        + [rows(8), whole((1, width)), whole((1, width))],
        out_specs=[rows(width)] * 4,
        out_shape=[
            jax.ShapeDtypeStruct((tokens, width), BF16),
            jax.ShapeDtypeStruct((tokens, width), F32),
            jax.ShapeDtypeStruct((tokens, width), F32),
            jax.ShapeDtypeStruct((tokens, width), BF16),
        ],
        scratch_shapes=[pltpu.VMEM((width, width), BF16)],
        compiler_params=pltpu.CompilerParams(
            dimension_semantics=("arbitrary",), vmem_limit_bytes=VMEM_BYTES
        ),
        cost_estimate=pl.CostEstimate(
            flops=4 * tokens * width * width, bytes_accessed=12 << 20, transcendentals=0
        ),
        name="mix",
    )(tok, *q, *num, *tot, *come, *wo, cols, gain, shift)


def gelu_pair(x):
    cdf = 0.5 + 0.5 * lax.erf(x * 0.7071067811865476)
    density = 0.3989422804014327 * jnp.exp(-0.5 * x * x)
    return x * cdf, cdf + x * density


def feed_kernel(blocks, resume, n2, dy, *refs):
    refs = list(refs)
    wh = [refs.pop(0) for _ in range(blocks)]
    wr = [refs.pop(0) for _ in range(blocks)]
    wo = [refs.pop(0) for _ in range(blocks)]
    if resume:
        branch_in, dn2_in = refs.pop(0), refs.pop(0)
    branch, dn2 = refs.pop(0), refs.pop(0)
    gwh = [refs.pop(0) for _ in range(blocks)]
    gwr = [refs.pop(0) for _ in range(blocks)]
    ghb = [refs.pop(0) for _ in range(blocks)]
    act, hg = refs
    tokens, width = n2.shape
    for b in range(blocks):
        hidden = wh[b].shape[1]
        bias = wo[b][PAIR : PAIR + 1, :].astype(F32)
        bias_grad = jnp.zeros((8, hidden), F32)
        for i in range(tokens // CHUNK):
            rows = slice(i * CHUNK, (i + 1) * CHUNK)
            pre = nn(n2[rows, :], wh[b][...]) + bias
            value, slope = gelu_pair(pre)
            act[rows, :] = value.astype(BF16)
            grad = nt(dy[rows, :], wr[b][...]) * slope
            low = grad.astype(BF16)
            hg[rows, :] = low
            bias_grad = bias_grad + jnp.sum(grad.reshape(CHUNK // 8, 8, hidden), axis=0)
            out = nn(act[rows, :], wr[b][...])
            back = nt(low, wh[b][...])
            if b > 0:
                out = out + branch[rows, :]
                back = back + dn2[rows, :]
            elif resume:
                out = out + branch_in[rows, :]
                back = back + dn2_in[rows, :]
            branch[rows, :] = out
            dn2[rows, :] = back
        gwr[b][...] = tn(act[...], dy[...]).astype(BF16)
        gwh[b][...] = tn(n2[...], hg[...]).astype(BF16)
        ghb[b][...] = bias_grad


def feed(n2, dy, wh, wr, wo, partial):
    tokens, width = n2.shape
    blocks, hidden = len(wh), wh[0].shape[1]
    resume = partial is not None
    arrays = [n2, dy, *wh, *wr, *wo] + (list(partial) if resume else [])
    out_shape = [jax.ShapeDtypeStruct((tokens, width), F32)] * 2
    out_shape += [jax.ShapeDtypeStruct((width, hidden), BF16)] * blocks
    out_shape += [jax.ShapeDtypeStruct((hidden, width), BF16)] * blocks
    out_shape += [jax.ShapeDtypeStruct((8, hidden), F32)] * blocks
    vmem = pl.BlockSpec(memory_space=pltpu.VMEM)
    out = pl.pallas_call(
        functools.partial(feed_kernel, blocks, resume),
        in_specs=[vmem] * len(arrays),
        out_specs=[vmem] * len(out_shape),
        out_shape=out_shape,
        scratch_shapes=[pltpu.VMEM((tokens, hidden), BF16)] * 2,
        compiler_params=pltpu.CompilerParams(vmem_limit_bytes=VMEM_BYTES),
        cost_estimate=pl.CostEstimate(
            flops=12 * tokens * width * hidden * blocks, bytes_accessed=16 << 20, transcendentals=0
        ),
        name="feed",
    )(*arrays)
    return out[:2], out[2 : 2 + blocks], out[2 + blocks : 2 + 2 * blocks], out[2 + 2 * blocks :]


def unmix_kernel(blocks, dn2, residual, dy, mixed, inv, *refs):
    refs = list(refs)
    wo = [refs.pop(0) for _ in range(blocks)]
    q = [refs.pop(0) for _ in range(blocks // 2)]
    cols, gain, rgrad_out, low_out, dw_out, tg_out, back_out, small_out, w_all, back, small = refs
    step, last = pl.program_id(0), pl.num_programs(0) - 1

    @pl.when(step == 0)
    def _():
        for b in range(blocks):
            w_all[b * PAIR : (b + 1) * PAIR, :] = wo[b][:PAIR, :]
        back[...] = jnp.zeros_like(back)
        small[...] = jnp.zeros_like(small)

    live = cols[:, LIVE : LIVE + 1]
    reads = cols[:, READ_HALF : READ_HALF + 1].astype(BF16)
    xhat, rstd = normalise(residual[...])
    grad = dn2[...]
    scaled = grad * gain[...].astype(F32)
    mean_one = jnp.mean(scaled, axis=-1, keepdims=True)
    mean_two = jnp.mean(scaled * xhat, axis=-1, keepdims=True)
    wide = dy[...].astype(F32)
    rgrad = wide + rstd * (scaled - mean_one - xhat * mean_two)
    rgrad_out[...] = rgrad
    eight = lambda x: jnp.sum(x.reshape(CHUNK // 8, 8, x.shape[1]), axis=0)
    small[0] += eight(grad * xhat)
    small[1] += eight(grad)
    small[2] += eight(wide)
    low = rgrad.astype(BF16)
    low_out[...] = low
    mgrad = nt(low, w_all[...]) * live
    sums = pair_mask(PAIR).astype(BF16)
    sums = jnp.concatenate([sums, sums], axis=0)
    block_diagonal = pair_mask(2 * PAIR)
    for b in range(blocks):
        lanes = slice(b * PAIR, (b + 1) * PAIR)
        one = mgrad[:, lanes]
        scale = inv[:, lanes]
        dw = (one * scale).astype(BF16)
        terms = one * mixed[:, lanes].astype(F32)
        high = terms.astype(BF16)
        rest = (terms - high.astype(F32)).astype(BF16)
        total = nn(jnp.concatenate([high, rest], axis=1), sums)
        tg = jnp.where(scale < 1.0, -total * scale, 0.0).astype(BF16)
        dw_out[:, lanes] = dw
        tg_out[:, lanes] = tg
        back[b] += tn(q[b // 2][b % 2] * reads, jnp.concatenate([dw, tg], axis=1))

    @pl.when(step == last)
    def _():
        for b in range(blocks):
            back_out[b ^ 1] = jnp.where(block_diagonal, back[b], 0.0).astype(BF16)
        small_out[...] = small[...]


def unmix(dn2, residual, dy, mixed, inv, wo, q, cols, gain):
    tokens, width = dy.shape
    blocks = len(wo)
    whole = lambda shape: pl.BlockSpec(shape, lambda i: (0,) * len(shape))
    rows = lambda n: pl.BlockSpec((CHUNK, n), lambda i: (i, 0))
    part = pl.BlockSpec((2, CHUNK, PAIR), lambda i: (0, i, 0))
    return pl.pallas_call(
        functools.partial(unmix_kernel, blocks),
        grid=(tokens // CHUNK,),
        in_specs=[rows(width)] * 5
        + [whole(wo[0].shape)] * blocks
        + [part] * (blocks // 2)
        + [rows(8), whole((1, width))],
        out_specs=[rows(width)] * 4 + [whole((blocks, PAIR, 2 * PAIR)), whole((3, 8, width))],
        out_shape=[
            jax.ShapeDtypeStruct((tokens, width), F32),
            jax.ShapeDtypeStruct((tokens, width), BF16),
            jax.ShapeDtypeStruct((tokens, width), BF16),
            jax.ShapeDtypeStruct((tokens, width), BF16),
            jax.ShapeDtypeStruct((blocks, PAIR, 2 * PAIR), BF16),
            jax.ShapeDtypeStruct((3, 8, width), F32),
        ],
        scratch_shapes=[
            pltpu.VMEM((width, width), BF16),
            pltpu.VMEM((blocks, PAIR, 2 * PAIR), F32),
            pltpu.VMEM((3, 8, width), F32),
        ],
        compiler_params=pltpu.CompilerParams(
            dimension_semantics=("arbitrary",), vmem_limit_bytes=VMEM_BYTES
        ),
        cost_estimate=pl.CostEstimate(
            flops=4 * tokens * width * width, bytes_accessed=14 << 20, transcendentals=0
        ),
        name="unmix",
    )(dn2, residual, dy, mixed, inv, *wo, *q, cols, gain)


def finish_kernel(blocks, residual, branch, bias, mixed, low, *refs):
    out, gwo = refs[0], refs[1:]
    out[...] = (residual[...] + branch[...] + bias[...].astype(F32)).astype(BF16)
    grad = tn(mixed[...], low[...]).astype(BF16)
    for b in range(blocks):
        gwo[b][...] = grad[b * PAIR : (b + 1) * PAIR, :]


def finish(residual, branch, bias, mixed, low, blocks):
    tokens, width = residual.shape
    vmem = pl.BlockSpec(memory_space=pltpu.VMEM)
    out = pl.pallas_call(
        functools.partial(finish_kernel, blocks),
        in_specs=[vmem] * 5,
        out_specs=[vmem] * (1 + blocks),
        out_shape=[jax.ShapeDtypeStruct((tokens, width), BF16)]
        + [jax.ShapeDtypeStruct((PAIR, width), BF16)] * blocks,
        compiler_params=pltpu.CompilerParams(vmem_limit_bytes=VMEM_BYTES),
        cost_estimate=pl.CostEstimate(
            flops=2 * tokens * width * width, bytes_accessed=8 << 20, transcendentals=0
        ),
        name="finish",
    )(residual, branch, bias, mixed, low)
    return out[0], out[1:]


def attend_back_kernel(blocks, dw, tg, gone, *refs):
    refs = list(refs)
    groups = blocks // 2
    q, k, v, held, far = ([refs.pop(0) for _ in range(groups)] for _ in range(5))
    cols, doc_row, grads, state = refs

    @pl.when(pl.program_id(0) == 0)
    def _():
        state[...] = gone[...].astype(F32) * cols[0:1, FIRST_HALF : FIRST_HALF + 1]

    reads = cols[:, READ_CHUNK : READ_CHUNK + 1]
    reads_far = cols[:, READ_HALF : READ_HALF + 1]
    in_last = cols[:, IN_LAST : IN_LAST + 1]
    carried = cols[0:1, CARRIED : CARRIED + 1]
    mask = allowed_mask(cols[:, DOC : DOC + 1], doc_row[...])
    here = head_lanes((CHUNK, PAIR))
    block_diagonal = pair_mask(2 * PAIR)
    ones = jnp.ones((CHUNK, PAIR), BF16)
    zeros = jnp.zeros((CHUNK, PAIR), BF16)
    share = 1.0 / HEAD_DIM
    for b in range(blocks):
        g, i = divmod(b, 2)
        lanes = slice(b * PAIR, (b + 1) * PAIR)
        qb, kb, vb = q[g][i], k[g][i], v[g][i]
        dwb, tgb = dw[:, lanes], tg[:, lanes]
        q_t, dw_t = qb.T, dwb.T
        value_ones = jnp.concatenate([vb, ones], axis=1)
        grad_wide = jnp.concatenate([dwb, tgb * share], axis=1)
        dq = reads * nt(grad_wide, held[g][0, i]) + reads_far * nt(grad_wide, far[g][i])
        dk_t, dv_t = [], []
        for h, own in enumerate((here, jnp.logical_not(here))):
            feats = slice(h * HEAD_DIM, (h + 1) * HEAD_DIM)
            scores = nt(jnp.where(own, qb, zeros), kb)
            scores = jnp.where(mask, scores, 0.0).astype(BF16)
            own_wide = jnp.concatenate([own, own], axis=1)
            sgrad = nt(jnp.where(own_wide, grad_wide, jnp.zeros_like(grad_wide)), value_ones)
            sgrad = jnp.where(mask, sgrad, 0.0).astype(BF16)
            dq = dq + nn(sgrad, jnp.where(own, kb, zeros))
            dk_t.append(nn(q_t[feats], sgrad))
            dv_t.append(nn(dw_t[feats], scores))
        low = state[b].astype(BF16)
        dk = jnp.concatenate(dk_t, axis=0).T
        dv = jnp.concatenate(dv_t, axis=0).T
        dk = dk + in_last * nt(jnp.concatenate([vb, ones * share], axis=1), low)
        dv = dv + in_last * nn(kb, low[:, :PAIR])
        grads[b, 0] = (dq * jnp.minimum(qb.astype(F32), 1.0)).astype(BF16)
        grads[b, 1] = (dk * jnp.minimum(kb.astype(F32), 1.0)).astype(BF16)
        grads[b, 2] = dv.astype(BF16)
        grown = tn(qb * reads.astype(BF16), jnp.concatenate([dwb, tgb], axis=1))
        state[b] = carried * state[b] + jnp.where(block_diagonal, grown, 0.0)


def attend_back(dw, tg, gone, q, k, v, held, far, cols, doc_row):
    tokens, width = dw.shape
    groups = len(q)
    blocks, chunks = 2 * groups, tokens // CHUNK
    whole = lambda shape: pl.BlockSpec(shape, lambda i: (0,) * len(shape))
    rows = lambda n: pl.BlockSpec((CHUNK, n), lambda i: (chunks - 1 - i, 0))
    part = pl.BlockSpec((2, CHUNK, PAIR), lambda i: (0, chunks - 1 - i, 0))
    return pl.pallas_call(
        functools.partial(attend_back_kernel, blocks),
        grid=(chunks,),
        in_specs=[rows(width)] * 2
        + [whole((blocks, PAIR, 2 * PAIR))]
        + [part] * (3 * groups)
        + [pl.BlockSpec((1, 2, PAIR, 2 * PAIR), lambda i: (chunks - 1 - i, 0, 0, 0))] * groups
        + [whole((2, PAIR, 2 * PAIR))] * groups
        + [rows(8), pl.BlockSpec((1, CHUNK), lambda i: (0, chunks - 1 - i))],
        out_specs=pl.BlockSpec((blocks, 3, CHUNK, PAIR), lambda i: (0, 0, chunks - 1 - i, 0)),
        out_shape=jax.ShapeDtypeStruct((blocks, 3, tokens, PAIR), BF16),
        scratch_shapes=[pltpu.VMEM((blocks, PAIR, 2 * PAIR), F32)],
        compiler_params=pltpu.CompilerParams(
            dimension_semantics=("arbitrary",), vmem_limit_bytes=VMEM_BYTES
        ),
        cost_estimate=pl.CostEstimate(
            flops=20 * tokens * width * CHUNK, bytes_accessed=8 << 20, transcendentals=0
        ),
        name="attend_back",
    )(dw, tg, gone, *q, *k, *v, *held, *far, cols, doc_row)


def project_back_kernel(n1, grads, *outs):
    for b, out in enumerate(outs):
        both = jnp.concatenate([grads[b, p] for p in range(3)], axis=1)
        grad = tn(n1[...], both).astype(BF16)
        for p in range(3):
            out[p] = grad[:, p * PAIR : (p + 1) * PAIR]


def project_back(n1, grads):
    tokens, width = n1.shape
    blocks = grads.shape[0]
    vmem = pl.BlockSpec(memory_space=pltpu.VMEM)
    return pl.pallas_call(
        project_back_kernel,
        in_specs=[vmem] * 2,
        out_specs=[vmem] * blocks,
        out_shape=[jax.ShapeDtypeStruct((3, width, PAIR), BF16)] * blocks,
        compiler_params=pltpu.CompilerParams(vmem_limit_bytes=VMEM_BYTES),
        cost_estimate=pl.CostEstimate(
            flops=6 * tokens * width * width, bytes_accessed=6 << 20, transcendentals=0
        ),
        name="project_back",
    )(n1, grads)


def input_back_kernel(blocks, tok, rgrad, grads, gain, *refs):
    w, (out, small_out, w_all, small) = refs[:blocks], refs[blocks:]
    step, last = pl.program_id(0), pl.num_programs(0) - 1

    @pl.when(step == 0)
    def _():
        for b in range(blocks):
            for p in range(3):
                at = (3 * b + p) * PAIR
                w_all[:, at : at + PAIR] = w[b][p]
        small[...] = jnp.zeros_like(small)

    both = jnp.concatenate([grads[b, p] for b in range(blocks) for p in range(3)], axis=1)
    grad = nt(both, w_all[...])
    xhat, rstd = normalise(tok[...].astype(F32))
    scaled = grad * gain[...].astype(F32)
    mean_one = jnp.mean(scaled, axis=-1, keepdims=True)
    mean_two = jnp.mean(scaled * xhat, axis=-1, keepdims=True)
    out[...] = rgrad[...] + rstd * (scaled - mean_one - xhat * mean_two)
    eight = lambda x: jnp.sum(x.reshape(CHUNK // 8, 8, x.shape[1]), axis=0)
    small[0] += eight(grad * xhat)
    small[1] += eight(grad)

    @pl.when(step == last)
    def _():
        small_out[...] = small[...]


def input_back(tok, rgrad, grads, gain, w):
    tokens, width = tok.shape
    blocks = len(w)
    whole = lambda shape: pl.BlockSpec(shape, lambda i: (0,) * len(shape))
    rows = lambda n: pl.BlockSpec((CHUNK, n), lambda i: (i, 0))
    return pl.pallas_call(
        functools.partial(input_back_kernel, blocks),
        grid=(tokens // CHUNK,),
        in_specs=[rows(width)] * 2
        + [pl.BlockSpec((blocks, 3, CHUNK, PAIR), lambda i: (0, 0, i, 0)), whole((1, width))]
        + [whole((3, width, PAIR))] * blocks,
        out_specs=[rows(width), whole((2, 8, width))],
        out_shape=[
            jax.ShapeDtypeStruct((tokens, width), F32),
            jax.ShapeDtypeStruct((2, 8, width), F32),
        ],
        scratch_shapes=[
            pltpu.VMEM((width, 3 * blocks * PAIR), BF16),
            pltpu.VMEM((2, 8, width), F32),
        ],
        compiler_params=pltpu.CompilerParams(
            dimension_semantics=("arbitrary",), vmem_limit_bytes=VMEM_BYTES
        ),
        cost_estimate=pl.CostEstimate(
            flops=6 * tokens * width * width, bytes_accessed=10 << 20, transcendentals=0
        ),
        name="input_back",
    )(tok, rgrad, grads, gain, *w)


def swap(x, axis, size, bit):
    return lax.ppermute(x, axis, [(i, i ^ bit) for i in range(size)])


def piece(x, index, count):
    rows = x.shape[0] // count
    return lax.dynamic_slice_in_dim(x, index * rows, rows, 0)


def sum_over_dp(x, count):
    me = lax.axis_index("dp")
    near, far = me % 2, me // 2
    rest = count // 2
    mine = piece(x, near, 2).astype(F32) + swap(piece(x, 1 - near, 2), "dp", count, 1).astype(F32)
    low = mine.astype(BF16)
    total = piece(low, far, rest).astype(F32)
    for s in range(1, rest):
        total = total + swap(piece(low, far ^ s, rest), "dp", count, 2 * s).astype(F32)
    own = total.astype(BF16)
    rows = own.shape[0]
    half = jnp.zeros((rest,) + own.shape, BF16)
    half = lax.dynamic_update_index_in_dim(half, own, far, 0)
    for s in range(1, rest):
        half = lax.dynamic_update_index_in_dim(half, swap(own, "dp", count, 2 * s), far ^ s, 0)
    half = half.reshape((rows * rest,) + own.shape[1:])
    other = swap(half, "dp", count, 1)
    return jnp.where(
        near == 0, jnp.concatenate([half, other]), jnp.concatenate([other, half])
    ).astype(F32)


def body(
    dp,
    head,
    tokens,
    doc_ids,
    pad_mask,
    norm1_gain,
    norm1_shift,
    w_qkv,
    w_out,
    norm2_gain,
    norm2_shift,
    w_hidden,
    hidden_bias,
    w_return,
    return_bias,
    out_grad,
):
    count, width = tokens.shape
    length = doc_ids.shape[1]
    halves = length // count
    me = lax.axis_index("head")
    row, place = me // halves, me % halves

    def gather(x):
        across = swap(x, "head", head, 2)
        return [x, swap(x, "head", head, 1), across, swap(across, "head", head, 1)]

    extra = jnp.concatenate([w_out, jnp.broadcast_to(hidden_bias[None], (16, width))])
    wq = gather(w_qkv)
    wo = gather(extra)
    wh = gather(w_hidden)
    wr = gather(w_return)

    docs_row = lax.dynamic_index_in_dim(doc_ids, row, 0, keepdims=False)
    docs = lax.dynamic_slice_in_dim(docs_row, place * count, count, 0)
    live = lax.dynamic_slice_in_dim(
        lax.dynamic_index_in_dim(pad_mask, row, 0, keepdims=False), place * count, count, 0
    ).astype(F32)
    edge = docs_row[count - 1]
    second = (place > 0).astype(F32)
    chunks = count // CHUNK
    in_chunks = docs.reshape(chunks, CHUNK)
    ends = in_chunks[:, -1]
    before = jnp.concatenate([jnp.full((1,), -1, jnp.int32), ends[:-1]])
    spread = lambda x: jnp.broadcast_to(x[:, None], (chunks, CHUNK)).reshape(count)
    flags = [
        docs.astype(F32),
        live,
        (docs == edge).astype(F32) * second,
        (in_chunks == before[:, None]).astype(F32).reshape(count),
        (in_chunks == ends[:, None]).astype(F32).reshape(count),
        spread((ends == before).astype(F32)),
        jnp.broadcast_to(1.0 - second, (count,)),
        jnp.zeros((count,), F32),
    ]
    cols = jnp.stack(flags, axis=1)
    doc_row = docs.astype(F32)[None]
    line = lambda x: x[None]

    n1, *near = attend(tokens, (line(norm1_gain), line(norm1_shift)), wq[:2], cols, doc_row)
    far = attend(n1, None, wq[2:], cols, doc_row)
    q, k, v, num, tot, held, last = zip(near, far)
    come = [swap(x, "head", head, 1) for x in last]
    mixed, inv, residual, n2 = mix(
        tokens, q, num, tot, come, wo, cols, line(norm2_gain), line(norm2_shift)
    )
    partial, gwh_a, gwr_a, ghb_a = feed(n2, out_grad, wh[:2], wr[:2], wo[:2], None)
    partial, gwh_b, gwr_b, ghb_b = feed(n2, out_grad, wh[2:], wr[2:], wo[2:], partial)
    branch, dn2 = partial
    rgrad, low, dw, tg, gone, small2 = unmix(
        dn2, residual, out_grad, mixed, inv, wo, q, cols, line(norm2_gain)
    )
    gone_in = swap(gone, "head", head, 1)
    output, gwo = finish(residual, branch, line(return_bias), mixed, low, head)
    pgrads = attend_back(dw, tg, gone_in, q, k, v, held, come, cols, doc_row)
    gq = project_back(n1, pgrads)
    tokens_grad, small1 = input_back(tokens, rgrad, pgrads, line(norm1_gain), wq)

    def share(blocks):
        first = lambda a, b: (a.astype(F32) + swap(b, "head", head, 1).astype(F32))
        mine = first(blocks[0], blocks[1])
        theirs = first(blocks[2], blocks[3]).astype(BF16)
        return (mine + swap(theirs, "head", head, 2).astype(F32)).astype(BF16)

    gwh = sum_over_dp(share([*gwh_a, *gwh_b]), dp)
    gwr = sum_over_dp(share([*gwr_a, *gwr_b]), dp)
    ghb = [jnp.sum(x, axis=0) for x in (*ghb_a, *ghb_b)]
    rest = [
        jnp.concatenate([a, jnp.broadcast_to(b[None].astype(BF16), (PAIR, width))])
        for a, b in zip(gwo, ghb)
    ]
    rest = sum_over_dp(share(rest), dp)
    gw_out, g_bias = rest[:PAIR], rest[PAIR]
    gq = sum_over_dp(share([x.reshape(3 * width, PAIR) for x in gq]), dp).reshape(3, width, PAIR)

    small = jnp.concatenate([jnp.sum(small1, axis=1), jnp.sum(small2, axis=1)])
    bit = 1
    while bit < head:
        small = small + swap(small, "head", head, bit)
        bit *= 2
    bit = 1
    while bit < dp:
        small = small + swap(small, "dp", dp, bit)
        bit *= 2
    return (
        output,
        tokens_grad,
        small[0],
        small[1],
        gq,
        gw_out,
        small[2],
        small[3],
        gwh,
        g_bias,
        gwr,
        small[4],
    )


def solution(mesh):
    return jax.shard_map(
        functools.partial(body, mesh.shape["dp"], mesh.shape["head"]),
        mesh=mesh,
        in_specs=(
            P(("dp", "head"), None),
            P("dp", None),
            P("dp", None),
            P(),
            P(),
            P(None, None, "head"),
            P("head", None),
            P(),
            P(),
            P(None, "head"),
            P("head"),
            P("head", None),
            P(),
            P(("dp", "head"), None),
        ),
        out_specs=(
            P(("dp", "head"), None),
            P(("dp", "head"), None),
            P(),
            P(),
            P(None, None, "head"),
            P("head", None),
            P(),
            P(),
            P(None, "head"),
            P("head"),
            P("head", None),
            P(),
        ),
        check_vma=False,
    )
```

time: 900 us -> 240 us (0.27)
  waiting for transfers between devices: 431 us -> 57.5 us
  matrix products: 176 us -> 0 us
  local copies, waits for them, and re-layouts: 130 us -> 14 us
  Pallas kernels: 0 us -> 87.9 us
  starting transfers between devices: 0.77 us -> 65.7 us
  other arithmetic: 76.3 us -> 12.3 us
  blocking collectives: 62.5 us -> 0 us
  between operations: 14.7 us -> 1.64 us
    reduce_scatter x4 -> x0, waiting for transfers between devices: 210 us -> none  [the longest x1 70.1 us: body(): lax.psum_scatter(jnp.dot(mixed, w_out, preferred_element_type=jnp.float32...]
    dot_general x60 -> x0, matrix products: 176 us -> none  [the longest x1 25.4 us: body(): jnp.einsum('td,fd->tf', grad_all, w_return, preferred_element_type=jnp.fl...]
    all_gather x4 -> x0, waiting for transfers between devices: 120 us -> none  [the longest x1 35.6 us: body(): normed1_all = lax.all_gather(normed1_low, 'head', axis=0, tiled=True)]
    psum x1 -> x0, waiting for transfers between devices: 100 us -> none  [body(): lax.psum((w_qkv_grad, w_out_grad, w_hidden_grad, hidden_bias_grad, w_retu...]
    pallas_call x0 -> x10, Pallas kernels: none -> 87.9 us  [the longest x2 23.3 us: feed(): pl.pallas_call(functools.partial(feed_kernel, blocks, resume), in_specs=[...]
    ppermute x0 -> x64, starting transfers between devices: none -> 65.7 us  [swap(): return lax.ppermute(x, axis, [(i, i ^ bit) for i in range(size)])]
    psum x2 -> x0, blocking collectives: 62.5 us -> none  [the longest x1 39.5 us: body(): lax.psum((norm1_gain_grad, norm1_shift_grad, norm2_gain_grad, norm2_shift...]
    ppermute x0 -> x64, waiting for transfers between devices: none -> 57.5 us  [swap(): return lax.ppermute(x, axis, [(i, i ^ bit) for i in range(size)])]
  transfers between devices with their start and end apart: 9 -> 64, of which waited for: 9 -> 18; matrix products, arithmetic and copies ran while one was open for 6% -> 9% of each run, Pallas kernels for 0% -> 18%
where the time goes in v1:
time: 240 us; the launch traced here: 239 us
  Pallas kernels  87.9 us (37%)
  starting transfers between devices  65.7 us (27%)
  waiting for transfers between devices  57.5 us (24%)
  local copies, waits for them, and re-layouts  14 us (6%)
  other arithmetic  12.3 us (5%)
    ppermute x64, starting transfers between devices, swap(): return lax.ppermute(x, axis, [(i, i ^ bit) for i in range(size)])  65.7 us
    ppermute x64, waiting for transfers between devices, swap(): return lax.ppermute(x, axis, [(i, i ^ bit) for i in range(size)])  57.5 us
    pallas_call x2, Pallas kernels, feed(): pl.pallas_call(functools.partial(feed_kernel, blocks, resume), in_specs=[...  23.3 us
    pallas_call x2, Pallas kernels, attend(): pl.pallas_call(functools.partial(attend_kernel, blocks, first), grid=(chu...  15.4 us
    pallas_call x1, Pallas kernels, attend_back(): pl.pallas_call(functools.partial(attend_back_kernel, blocks), grid=(chunk...  14.4 us
    pallas_call x1, Pallas kernels, unmix(): pl.pallas_call(functools.partial(unmix_kernel, blocks), grid=(tokens // C...  10.3 us
    pallas_call x1, Pallas kernels, mix(): pl.pallas_call(functools.partial(mix_kernel, groups), grid=(tokens // CHU...  7.18 us
    pallas_call x1, Pallas kernels, input_back(): pl.pallas_call(functools.partial(input_back_kernel, blocks), grid=(tokens...  7.04 us
  transfers between devices with their start and end apart: 64, of which 18 were waited for; matrix products, arithmetic and copies ran while one was open for 9% of the time, Pallas kernels for 18%

profile of v1, /device:TPU:0, one launch (start us, length us, event | category | flops | bytes accessed | tf_op | source)
XLA Modules:
  0.0 238.9 jit_solution(4050265386967214581)
XLA Ops:
  1.2 2.6 %collective-permute-start.1 = (bf16[3,512,128]{2,1,0:T(8,128)(2,1)}, bf16[3,512,128]{2,1,0:T(8,128)(2,1)S(1)}, u32[]{:S(2)}, u32[]{:S(2)}) collective-permute-start(bf16[3,512,128]{2,1,0:T(8,128)(2,1)} %refs_0_.5), channel_id=1, source_target_pairs={{0,2},{1,3},{2,0},{3,1},{4,6},{5,7},{6,4},{7,5},{8,10},{9,11},{10,... | collective-permute-start | bytes 1179656 | tf_op jit(solution)/shard_map/ppermute | solution.py:574
  5.7 1.8 collective-permute-start.10
  7.5 1.4 dynamic-slice_convert_fusion
  10.4 6.7 %collective-permute-done.6.refs_10_.refs_4_.refs_2_ = bf16[144,512]{1,0:T(8,128)(2,1)S(1)} collective-permute-done((bf16[144,512]{1,0:T(8,128)(2,1)S(1)}, bf16[144,512]{1,0:T(8,128)(2,1)S(1)}, u32[]{:S(2)}, u32[]{:S(2)}) %collective-permute-start.6) | collective-permute-done | bytes 147488 | tf_op jit(solution)/shard_map/ppermute | solution.py:574
  17.7 1.9 collective-permute-start.8
  20.4 1.3 dynamic-slice.2
  22.2 1.4 compare_select_fusion
  23.7 1.0 copy.49.refs_5_.refs_3_.refs_12_.refs_6_.refs_10_
  24.7 1.3 broadcast_in_dim.117.refs_1_.gain
  26.0 1.3 broadcast_in_dim.118.refs_2_
  27.3 8.1 %attend.2 = (bf16[1024,512]{1,0:T(8,128)(2,1)}, bf16[2,1024,128]{2,1,0:T(8,128)(2,1)}, bf16[2,1024,128]{2,1,0:T(8,128)(2,1)}, bf16[2,1024,128]{2,1,0:T(8,128)(2,...) custom-call(bf16[1024,512]{1,0:T(8,128)(2,1)} %tok.3, ...), custom_call_target="tpu_custom_call" | custom-call | flops 1342177280 | bytes 8388608 | tf_op jit(solution)/shard_map/attend/pallas_call | solution.py:136
  36.1 7.4 %attend.3 = (bf16[2,1024,128]{2,1,0:T(8,128)(2,1)}, bf16[2,1024,128]{2,1,0:T(8,128)(2,1)}, bf16[2,1024,128]{2,1,0:T(8,128)(2,1)}, f32[2,1024,128]{2,1,0:T(8,128)...) custom-call(bf16[1024,512]{1,0:T(8,128)(2,1)} %get-tuple-element.65.refs_0_.n1, ...), custom_call_target="tpu_custom_call" | custom-call | flops 1342177280 | bytes 8388608 | tf_op jit(solution)/shard_map/attend/pallas_call | solution.py:136
  46.1 7.2 %mix.1 = (bf16[1024,512]{1,0:T(8,128)(2,1)}, f32[1024,512]{1,0:T(8,128)}, f32[1024,512]{1,0:T(8,128)}, bf16[1024,512]{1,0:T(8,128)(2,1)}) custom-call(bf16[1024,512]{1,0:T(8,128)(2,1)} %tok.3, bf16[2,1024,128]{2,1,0:T(8,128)(2,1)} %get-tuple-element.64.refs_0_.refs_4_, bf16[2,1024,128]{2,1,0:T(8,128)(2,1)} %get-tuple-element.66.refs_1_.refs_5_, ...), custom_call_target="tpu_custom_call" | custom-call | flops 1073741824 | bytes 12582912 | tf_op jit(solution)/shard_map/mix/pallas_call | solution.py:193
  54.1 11.0 %feed.2 = (f32[1024,512]{1,0:T(8,128)}, f32[1024,512]{1,0:T(8,128)}, bf16[512,512]{1,0:T(8,128)(2,1)}, bf16[512,512]{1,0:T(8,128)(2,1)}, bf16[512,512]{1,0:T(8,1...) custom-call(bf16[1024,512]{1,0:T(8,128)(2,1)} %get-tuple-element.74.n2, ...), custom_call_target="tpu_custom_call" | custom-call | flops 6442450944 | bytes 16777216 | tf_op jit(solution)/shard_map/feed/pallas_call | solution.py:276
  66.1 12.3 %feed.3 = (f32[1024,512]{1,0:T(8,128)}, f32[1024,512]{1,0:T(8,128)}, bf16[512,512]{1,0:T(8,128)(2,1)}, bf16[512,512]{1,0:T(8,128)(2,1)}, bf16[512,512]{1,0:T(8,1...) custom-call(bf16[1024,512]{1,0:T(8,128)(2,1)} %get-tuple-element.74.n2, ...), custom_call_target="tpu_custom_call" | custom-call | flops 6442450944 | bytes 16777216 | tf_op jit(solution)/shard_map/feed/pallas_call | solution.py:276
  78.4 10.3 %unmix.1 = (f32[1024,512]{1,0:T(8,128)}, bf16[1024,512]{1,0:T(8,128)(2,1)}, bf16[1024,512]{1,0:T(8,128)(2,1)}, bf16[1024,512]{1,0:T(8,128)(2,1)}, bf16[4,128,256]{2,1,0:T(8,128)(2,1)}, /*index=5*/f32[3,8,512]{2,1,0:T(8,128)}) custom-call(f32[1024,512]{1,0:T(8,128)} %get-tuple-element.79.dn2, f32[1024,512]{1,0:T(8,128)} %get-tuple-element.73.residual, ...), custom_call_target="tpu_custom_call" | custom-call | flops 1073741824 | bytes 14680064 | tf_op jit(solution)/shard_map/unmix/pallas_call | solution.py:352
  90.5 4.9 %finish.1 = (bf16[1024,512]{1,0:T(8,128)(2,1)}, bf16[128,512]{1,0:T(8,128)(2,1)}, bf16[128,512]{1,0:T(8,128)(2,1)}, bf16[128,512]{1,0:T(8,128)(2,1)}, bf16[128,512]{1,0:T(8,128)(2,1)}) custom-call(f32[1024,512]{1,0:T(8,128)} %get-tuple-element.73.residual, f32[1024,512]{1,0:T(8,128)} %get-tuple-element.77.branch, bf16[1,512]{1,0:T(2,128)(2,1)} %broadcast_in_dim.125.bias, ...), custom_call_target="tpu_custom_call" | custom-call | flops 536870912 | bytes 8388608 | tf_op jit(solution)/shard_map/finish/pallas_call | solution.py:394
  96.1 14.4 %attend_back.1.grads = bf16[4,3,1024,128]{3,2,1,0:T(8,128)(2,1)} custom-call(bf16[1024,512]{1,0:T(8,128)(2,1)} %get-tuple-element.84.dw, bf16[1024,512]{1,0:T(8,128)(2,1)} %get-tuple-element.85.tg, bf16[4,128,256]{2,1,0:T(8,128)(2,1)} %copy-done.15, bf16[2,1024,128]{2,1,0:T(8,128)(2,1)} %get-tuple-element.64.refs_0_.refs_4_, ...), custom_call_target="tpu_custom_call" | custom-call | flops 2684354560 | bytes 8388608 | tf_op jit(solution)/shard_map/attend_back/pallas_call | solution.py:468
  110.6 7.0 %input_back.1 = (f32[1024,512]{1,0:T(8,128)}, f32[2,8,512]{2,1,0:T(8,128)}) custom-call(bf16[1024,512]{1,0:T(8,128)(2,1)} %tok.3, f32[1024,512]{1,0:T(8,128)} %get-tuple-element.83.rgrad, bf16[4,3,1024,128]{3,2,1,0:T(8,128)(2,1)} %attend_back.1.grads, bf16[1,512]{1,0:T(2,128)(2,1)} %broadcast_in_dim.117.refs_1_.gain, bf16[3,512,128]{2,1,0:T(8,128)(2,1)} %refs_0_.5, ...), custom_call_target="tpu_custom_call" | custom-call | flops 1610612736 | bytes 10485760 | tf_op jit(solution)/shard_map/input_back/pallas_call | solution.py:548
  120.6 2.9 %collective-permute-done.16 = f32[5,512]{1,0:T(8,128)S(1)} collective-permute-done((f32[5,512]{1,0:T(8,128)S(1)}, f32[5,512]{1,0:T(8,128)S(1)}, u32[]{:S(2)}, u32[]{:S(2)}) %collective-permute-start.16) | collective-permute-done | bytes 10272 | tf_op jit(solution)/shard_map/ppermute | solution.py:574
  123.5 1.5 collective-permute-start.17
  125.1 2.1 collective-permute-done.17
  127.2 1.6 collective-permute-start.18
  129.4 1.5 collective-permute-done.18
  131.0 2.7 %collective-permute-start.19 = (f32[5,512]{1,0:T(8,128)S(1)}, f32[5,512]{1,0:T(8,128)S(1)}, u32[]{:S(2)}, u32[]{:S(2)}) collective-permute-start(f32[5,512]{1,0:T(8,128)S(1)} %add.217), channel_id=1, source_target_pairs={{0,16},{4,20},{8,24},{12,28},{16,0},{20,4},{24,8},{28,12},{1,17},{... | collective-permute-start | bytes 30728 | tf_op jit(solution)/shard_map/ppermute | solution.py:574
  133.7 5.4 %project_back.1 = (bf16[3,512,128]{2,1,0:T(8,128)(2,1)}, bf16[3,512,128]{2,1,0:T(8,128)(2,1)}, bf16[3,512,128]{2,1,0:T(8,128)(2,1)}, bf16[3,512,128]{2,1,0:T(8,128)(2,1)}) custom-call(bf16[1024,512]{1,0:T(8,128)(2,1)} %get-tuple-element.65.refs_0_.n1, bf16[4,3,1024,128]{3,2,1,0:T(8,128)(2,1)} %attend_back.1.grads), custom_call_target="tpu_custom_call" | custom-call | flops 1610612736 | bytes 6291456 | tf_op jit(solution)/shard_map/project_back/pallas_call | solution.py:502
  140.5 1.5 collective-permute-start.34
  142.1 3.9 %collective-permute-done.34 = bf16[128,512]{1,0:T(8,128)(2,1)S(1)} collective-permute-done((bf16[128,512]{1,0:T(8,128)(2,1)S(1)}, bf16[128,512]{1,0:T(8,128)(2,1)S(1)}, u32[]{:S(2)}, u32[]{:S(2)}) %collective-permute-start.34) | collective-permute-done | bytes 131104 | tf_op jit(solution)/shard_map/ppermute | solution.py:574
  146.0 1.5 collective-permute-start.35
  147.9 2.6 %collective-permute-start.37 = (bf16[32,512]{1,0:T(8,128)(2,1)S(1)}, bf16[32,512]{1,0:T(8,128)(2,1)S(1)}, u32[]{:S(2)}, u32[]{:S(2)}) collective-permute-start(bf16[32,512]{1,0:T(8,128)(2,1)S(1)} %get-tuple-element.134), channel_id=1, source_target_pairs={{0,24},{4,28},{8,16},{12,20},{16,8},{20,12},{24,0},{28,4},{1,25},{... | collective-permute-start | bytes 98312 | tf_op jit(solution)/shard_map/ppermute | solution.py:574
  150.7 2.0 collective-permute-done.36
  154.4 3.8 %collective-permute-done.38 = bf16[32,512]{1,0:T(8,128)(2,1)S(1)} collective-permute-done((bf16[32,512]{1,0:T(8,128)(2,1)S(1)}, bf16[32,512]{1,0:T(8,128)(2,1)S(1)}, u32[]{:S(2)}, u32[]{:S(2)}) %collective-permute-start.38) | collective-permute-done | bytes 32800 | tf_op jit(solution)/shard_map/ppermute | solution.py:574
  158.2 1.1 collective-permute-start.39
  159.3 4.1 %collective-permute-done.39 = bf16[32,512]{1,0:T(8,128)(2,1)S(1)} collective-permute-done((bf16[32,512]{1,0:T(8,128)(2,1)S(1)}, bf16[32,512]{1,0:T(8,128)(2,1)S(1)}, u32[]{:S(2)}, u32[]{:S(2)}) %collective-permute-start.39) | collective-permute-done | bytes 32800 | tf_op jit(solution)/shard_map/ppermute | solution.py:574
  163.4 2.5 %collective-permute-start.40 = (bf16[32,512]{1,0:T(8,128)(2,1)S(1)}, bf16[32,512]{1,0:T(8,128)(2,1)S(1)}, u32[]{:S(2)}, u32[]{:S(2)}) collective-permute-start(bf16[32,512]{1,0:T(8,128)(2,1)S(1)} %get-tuple-element.121), channel_id=1, source_target_pairs={{0,24},{4,28},{8,16},{12,20},{16,8},{20,12},{24,0},{28,4},{1,25},{... | collective-permute-start | bytes 98312 | tf_op jit(solution)/shard_map/ppermute | solution.py:574
  165.9 3.2 %collective-permute-done.40 = bf16[32,512]{1,0:T(8,128)(2,1)S(1)} collective-permute-done((bf16[32,512]{1,0:T(8,128)(2,1)S(1)}, bf16[32,512]{1,0:T(8,128)(2,1)S(1)}, u32[]{:S(2)}, u32[]{:S(2)}) %collective-permute-start.40) | collective-permute-done | bytes 32800 | tf_op jit(solution)/shard_map/ppermute | solution.py:574
  169.1 1.8 collective-permute-start.55
  171.2 1.4 collective-permute-start.41
  173.6 13.4 %collective-permute-done.22 = bf16[1536,128]{1,0:T(8,128)(2,1)S(1)} collective-permute-done((bf16[1536,128]{1,0:T(8,128)(2,1)S(1)}, bf16[1536,128]{1,0:T(8,128)(2,1)S(1)}, u32[]{:S(2)}, u32[]{:S(2)}) %collective-permute-start.22) | collective-permute-done | bytes 393248 | tf_op jit(solution)/shard_map/ppermute | solution.py:574
  187.2 1.5 collective-permute-start.23
  189.6 3.3 %collective-permute-done.23 = bf16[768,128]{1,0:T(8,128)(2,1)S(1)} collective-permute-done((bf16[768,128]{1,0:T(8,128)(2,1)S(1)}, bf16[768,128]{1,0:T(8,128)(2,1)S(1)}, u32[]{:S(2)}, u32[]{:S(2)}) %collective-permute-start.23) | collective-permute-done | bytes 196640 | tf_op jit(solution)/shard_map/ppermute | solution.py:574
  193.2 1.0 collective-permute-start.25
  194.2 3.3 %collective-permute-start.26 = (bf16[192,128]{1,0:T(8,128)(2,1)S(1)}, bf16[192,128]{1,0:T(8,128)(2,1)S(1)}, u32[]{:S(2)}, u32[]{:S(2)}) collective-permute-start(bf16[192,128]{1,0:T(8,128)(2,1)S(1)} %get-tuple-element.131), channel_id=1, source_target_pairs={{0,24},{4,28},{8,16},{12,20},{16,8},{20,12},{24,0},{28,4},{1,25},{... | collective-permute-start | bytes 147464 | tf_op jit(solution)/shard_map/ppermute | solution.py:574
  198.9 2.0 collective-permute-done.25
  201.0 2.4 collective-permute-start.27
  204.1 1.7 collective-permute-start.29
  206.0 1.1 collective-permute-start.57
  207.1 1.7 collective-permute-start.58
  208.8 1.7 collective-permute-start.59
  210.8 2.7 %collective-permute-start.47 = (bf16[64,512]{1,0:T(8,128)(2,1)S(1)}, bf16[64,512]{1,0:T(8,128)(2,1)S(1)}, u32[]{:S(2)}, u32[]{:S(2)}) collective-permute-start(bf16[64,512]{1,0:T(8,128)(2,1)S(1)} %get-tuple-element.129), channel_id=1, source_target_pairs={{0,16},{4,20},{8,24},{12,28},{16,0},{20,4},{24,8},{28,12},{1,17},{... | collective-permute-start | bytes 196616 | tf_op jit(solution)/shard_map/ppermute | solution.py:574
  213.4 1.7 collective-permute-start.48
  215.6 1.6 collective-permute-start.30
  217.3 1.9 collective-permute-start.60
  219.6 1.0 collective-permute-done.47
  220.6 1.8 collective-permute-start.62
  222.9 2.3 collective-permute-start.50
  225.2 1.8 collective-permute-start.51
  227.0 1.3 collective-permute-start.63
  228.4 2.9 %collective-permute-done.51 = bf16[64,512]{1,0:T(8,128)(2,1)S(1)} collective-permute-done((bf16[64,512]{1,0:T(8,128)(2,1)S(1)}, bf16[64,512]{1,0:T(8,128)(2,1)S(1)}, u32[]{:S(2)}, u32[]{:S(2)}) %collective-permute-start.51) | collective-permute-done | bytes 65568 | tf_op jit(solution)/shard_map/ppermute | solution.py:574
  231.3 1.5 collective-permute-start.52
  232.9 0.9 convert.6
  233.9 1.2 fusion.4
  235.1 2.7 %collective-permute-done.52 = bf16[256,512]{1,0:T(8,128)(2,1)S(1)} collective-permute-done((bf16[256,512]{1,0:T(8,128)(2,1)S(1)}, bf16[256,512]{1,0:T(8,128)(2,1)S(1)}, u32[]{:S(2)}, u32[]{:S(2)}) %collective-permute-start.52) | collective-permute-done | bytes 262176 | tf_op jit(solution)/shard_map/ppermute | solution.py:574
  237.7 1.2 fusion.3
  (238 shorter events, 27.7 us)
Async XLA Ops:
  0.6 21.0 %collective-permute-start = (bf16[3,512,128]{2,1,0:T(8,128)(2,1)}, bf16[3,512,128]{2,1,0:T(8,128)(2,1)S(1)}, u32[]{:S(2)}, u32[]{:S(2)}) collective-permute-start(bf16[3,512,128]{2,1,0:T(8,128)(2,1)} %refs_0_.5), channel_id=1, source_target_pairs={{0,1},{1,0},{2,3},{3,2},{4,5},{5,4},{6,7},{7,6},{8,9},{9,8},{10,11... | collective-permute-start | bytes 1179656 | tf_op jit(solution)/shard_map/ppermute | solution.py:574
  1.2 15.9 %collective-permute-start.1 = (bf16[3,512,128]{2,1,0:T(8,128)(2,1)}, bf16[3,512,128]{2,1,0:T(8,128)(2,1)S(1)}, u32[]{:S(2)}, u32[]{:S(2)}) collective-permute-start(bf16[3,512,128]{2,1,0:T(8,128)(2,1)} %refs_0_.5), channel_id=1, source_target_pairs={{0,2},{1,3},{2,0},{3,1},{4,6},{5,7},{6,4},{7,5},{8,10},{9,11},{10,... | collective-permute-start | bytes 1179656 | tf_op jit(solution)/shard_map/ppermute | solution.py:574
  5.4 11.7 %collective-permute-start.6 = (bf16[144,512]{1,0:T(8,128)(2,1)S(1)}, bf16[144,512]{1,0:T(8,128)(2,1)S(1)}, u32[]{:S(2)}, u32[]{:S(2)}) collective-permute-start(bf16[144,512]{1,0:T(8,128)(2,1)S(1)} %pad_maximum_fusion.2.refs_8_.refs_4_.refs_0_), channel_id=1, source_target_pairs={{0,2},{1,3},{2,0},{3,1},{4,6},{5,7},{6,4},{7,5},{8,10},{9,11},{10,... | collective-permute-start | bytes 442376 | tf_op jit(solution)/shard_map/ppermute | solution.py:574
  5.4 12.2 %collective-permute-start.5 = (bf16[144,512]{1,0:T(8,128)(2,1)S(1)}, bf16[144,512]{1,0:T(8,128)(2,1)S(1)}, u32[]{:S(2)}, u32[]{:S(2)}) collective-permute-start(bf16[144,512]{1,0:T(8,128)(2,1)S(1)} %pad_maximum_fusion.2.refs_8_.refs_4_.refs_0_), channel_id=1, source_target_pairs={{0,1},{1,0},{2,3},{3,2},{4,5},{5,4},{6,7},{7,6},{8,9},{9,8},{10,11... | collective-permute-start | bytes 442376 | tf_op jit(solution)/shard_map/ppermute | solution.py:574
  5.7 39.2 %collective-permute-start.10 = (bf16[512,512]{1,0:T(8,128)(2,1)}, bf16[512,512]{1,0:T(8,128)(2,1)S(1)}, u32[]{:S(2)}, u32[]{:S(2)}) collective-permute-start(bf16[512,512]{1,0:T(8,128)(2,1)} %refs_2_.1), channel_id=1, source_target_pairs={{0,2},{1,3},{2,0},{3,1},{4,6},{5,7},{6,4},{7,5},{8,10},{9,11},{10,... | collective-permute-start | bytes 1572872 | tf_op jit(solution)/shard_map/ppermute | solution.py:574
  17.1 4.6 %collective-permute-start.7 = (bf16[144,512]{1,0:T(8,128)(2,1)S(1)}, bf16[144,512]{1,0:T(8,128)(2,1)S(1)}, u32[]{:S(2)}, u32[]{:S(2)}) collective-permute-start(bf16[144,512]{1,0:T(8,128)(2,1)S(1)} %collective-permute-done.6.refs_10_.refs_4_.refs_2_), channel_id=1, source_target_pairs={{0,1},{1,0},{2,3},{3,2},{4,5},{5,4},{6,7},{7,6},{8,9},{9,8},{10,11... | collective-permute-start | bytes 442376 | tf_op jit(solution)/shard_map/ppermute | solution.py:574
  17.1 18.3 %collective-permute-start.2 = (bf16[3,512,128]{2,1,0:T(8,128)(2,1)S(1)}, bf16[3,512,128]{2,1,0:T(8,128)(2,1)S(1)}, u32[]{:S(2)}, u32[]{:S(2)}) collective-permute-start(bf16[3,512,128]{2,1,0:T(8,128)(2,1)S(1)} %collective-permute-done.1.refs_1_.refs_2_), channel_id=1, source_target_pairs={{0,1},{1,0},{2,3},{3,2},{4,5},{5,4},{6,7},{7,6},{8,9},{9,8},{10,11... | collective-permute-start | bytes 1179656 | tf_op jit(solution)/shard_map/ppermute | solution.py:574
  17.7 27.6 %collective-permute-start.8 = (bf16[512,512]{1,0:T(8,128)(2,1)}, bf16[512,512]{1,0:T(8,128)(2,1)S(1)}, u32[]{:S(2)}, u32[]{:S(2)}) collective-permute-start(bf16[512,512]{1,0:T(8,128)(2,1)} %refs_0_.4), channel_id=1, source_target_pairs={{0,2},{1,3},{2,0},{3,1},{4,6},{5,7},{6,4},{7,5},{8,10},{9,11},{10,... | collective-permute-start | bytes 1572872 | tf_op jit(solution)/shard_map/ppermute | solution.py:574
  21.7 31.6 %collective-permute-start.12 = (bf16[512,512]{1,0:T(8,128)(2,1)}, bf16[512,512]{1,0:T(8,128)(2,1)S(1)}, u32[]{:S(2)}, u32[]{:S(2)}) collective-permute-start(bf16[512,512]{1,0:T(8,128)(2,1)} %refs_0_.4), channel_id=1, source_target_pairs={{0,1},{1,0},{2,3},{3,2},{4,5},{5,4},{6,7},{7,6},{8,9},{9,8},{10,11... | collective-permute-start | bytes 1572872 | tf_op jit(solution)/shard_map/ppermute | solution.py:574
  21.7 31.6 %collective-permute-start.13 = (bf16[512,512]{1,0:T(8,128)(2,1)}, bf16[512,512]{1,0:T(8,128)(2,1)}, u32[]{:S(2)}, u32[]{:S(2)}) collective-permute-start(bf16[512,512]{1,0:T(8,128)(2,1)} %refs_2_.1), channel_id=1, source_target_pairs={{0,1},{1,0},{2,3},{3,2},{4,5},{5,4},{6,7},{7,6},{8,9},{9,8},{10,11... | collective-permute-start | bytes 1572872 | tf_op jit(solution)/shard_map/ppermute | solution.py:574
  35.4 8.1 %collective-permute-start.3 = (bf16[2,128,256]{2,1,0:T(8,128)(2,1)}, bf16[2,128,256]{2,1,0:T(8,128)(2,1)S(1)}, u32[]{:S(2)}, u32[]{:S(2)}) collective-permute-start(bf16[2,128,256]{2,1,0:T(8,128)(2,1)} %get-tuple-element.71), channel_id=1, source_target_pairs={{0,1},{1,0},{2,3},{3,2},{4,5},{5,4},{6,7},{7,6},{8,9},{9,8},{10,11... | collective-permute-start | bytes 393224 | tf_op jit(solution)/shard_map/ppermute | solution.py:574
  43.5 1.9 collective-permute-start.4
  44.9 20.2 %collective-permute-start.11 = (bf16[512,512]{1,0:T(8,128)(2,1)S(1)}, bf16[512,512]{1,0:T(8,128)(2,1)S(1)}, u32[]{:S(2)}, u32[]{:S(2)}) collective-permute-start(bf16[512,512]{1,0:T(8,128)(2,1)S(1)} %collective-permute-done.10.refs_2_), channel_id=1, source_target_pairs={{0,1},{1,0},{2,3},{3,2},{4,5},{5,4},{6,7},{7,6},{8,9},{9,8},{10,11... | collective-permute-start | bytes 1572872 | tf_op jit(solution)/shard_map/ppermute | solution.py:574
  45.3 19.9 %collective-permute-start.9 = (bf16[512,512]{1,0:T(8,128)(2,1)S(1)}, bf16[512,512]{1,0:T(8,128)(2,1)S(1)}, u32[]{:S(2)}, u32[]{:S(2)}) collective-permute-start(bf16[512,512]{1,0:T(8,128)(2,1)S(1)} %collective-permute-done.8.refs_0_), channel_id=1, source_target_pairs={{0,1},{1,0},{2,3},{3,2},{4,5},{5,4},{6,7},{7,6},{8,9},{9,8},{10,11... | collective-permute-start | bytes 1572872 | tf_op jit(solution)/shard_map/ppermute | solution.py:574
  88.7 6.7 %collective-permute-start.14 = (bf16[4,128,256]{2,1,0:T(8,128)(2,1)}, bf16[4,128,256]{2,1,0:T(8,128)(2,1)S(1)}, u32[]{:S(2)}, u32[]{:S(2)}) collective-permute-start(bf16[4,128,256]{2,1,0:T(8,128)(2,1)} %get-tuple-element.86), channel_id=1, source_target_pairs={{0,1},{1,0},{2,3},{3,2},{4,5},{5,4},{6,7},{7,6},{8,9},{9,8},{10,11... | collective-permute-start | bytes 786440 | tf_op jit(solution)/shard_map/ppermute | solution.py:574
  118.4 1.2 collective-permute-start.15
  118.7 10.0 %collective-permute-start.32 = (bf16[256,512]{1,0:T(8,128)(2,1)S(1)}, bf16[256,512]{1,0:T(8,128)(2,1)S(1)}, u32[]{:S(2)}, u32[]{:S(2)}) collective-permute-start(bf16[256,512]{1,0:T(8,128)(2,1)S(1)} %pad_maximum_fusion.1), channel_id=1, source_target_pairs={{0,1},{1,0},{2,3},{3,2},{4,5},{5,4},{6,7},{7,6},{8,9},{9,8},{10,11... | collective-permute-start | bytes 786440 | tf_op jit(solution)/shard_map/ppermute | solution.py:574
  119.6 3.8 %collective-permute-start.16 = (f32[5,512]{1,0:T(8,128)S(1)}, f32[5,512]{1,0:T(8,128)S(1)}, u32[]{:S(2)}, u32[]{:S(2)}) collective-permute-start(f32[5,512]{1,0:T(8,128)S(1)} %fusion.6), channel_id=1, source_target_pairs={{0,2},{1,3},{2,0},{3,1},{4,6},{5,7},{6,4},{7,5},{8,10},{9,11},{10,... | collective-permute-start | bytes 30728 | tf_op jit(solution)/shard_map/ppermute | solution.py:574
  119.9 51.0 %collective-permute-start.42 = (bf16[512,512]{1,0:T(8,128)(2,1)S(1)}, bf16[512,512]{1,0:T(8,128)(2,1)S(1)}, u32[]{:S(2)}, u32[]{:S(2)}) collective-permute-start(bf16[512,512]{1,0:T(8,128)(2,1)S(1)} %copy-done.28), channel_id=1, source_target_pairs={{0,1},{1,0},{2,3},{3,2},{4,5},{5,4},{6,7},{7,6},{8,9},{9,8},{10,11... | collective-permute-start | bytes 1572872 | tf_op jit(solution)/shard_map/ppermute | solution.py:574
  120.2 21.7 %collective-permute-start.43 = (bf16[512,512]{1,0:T(8,128)(2,1)}, bf16[512,512]{1,0:T(8,128)(2,1)S(1)}, u32[]{:S(2)}, u32[]{:S(2)}) collective-permute-start(bf16[512,512]{1,0:T(8,128)(2,1)} %get-tuple-element.111), channel_id=1, source_target_pairs={{0,1},{1,0},{2,3},{3,2},{4,5},{5,4},{6,7},{7,6},{8,9},{9,8},{10,11... | collective-permute-start | bytes 1572872 | tf_op jit(solution)/shard_map/ppermute | solution.py:574
  123.5 3.7 %collective-permute-start.17 = (f32[5,512]{1,0:T(8,128)S(1)}, f32[5,512]{1,0:T(8,128)S(1)}, u32[]{:S(2)}, u32[]{:S(2)}) collective-permute-start(f32[5,512]{1,0:T(8,128)S(1)} %add.215), channel_id=1, source_target_pairs={{0,4},{4,0},{8,12},{12,8},{16,20},{20,16},{24,28},{28,24},{1,5},{5... | collective-permute-start | bytes 30728 | tf_op jit(solution)/shard_map/ppermute | solution.py:574
  125.0 14.8 %collective-permute-start.31 = (bf16[256,512]{1,0:T(8,128)(2,1)S(1)}, bf16[256,512]{1,0:T(8,128)(2,1)S(1)}, u32[]{:S(2)}, u32[]{:S(2)}) collective-permute-start(bf16[256,512]{1,0:T(8,128)(2,1)S(1)} %pad_maximum_fusion), channel_id=1, source_target_pairs={{0,1},{1,0},{2,3},{3,2},{4,5},{5,4},{6,7},{7,6},{8,9},{9,8},{10,11... | collective-permute-start | bytes 786440 | tf_op jit(solution)/shard_map/ppermute | solution.py:574
  127.2 3.7 %collective-permute-start.18 = (f32[5,512]{1,0:T(8,128)S(1)}, f32[5,512]{1,0:T(8,128)S(1)}, u32[]{:S(2)}, u32[]{:S(2)}) collective-permute-start(f32[5,512]{1,0:T(8,128)S(1)} %add.216), channel_id=1, source_target_pairs={{0,8},{4,12},{8,0},{12,4},{16,24},{20,28},{24,16},{28,20},{1,9},{5... | collective-permute-start | bytes 30728 | tf_op jit(solution)/shard_map/ppermute | solution.py:574
  128.9 11.4 %collective-permute-start.33 = (bf16[256,512]{1,0:T(8,128)(2,1)S(1)}, bf16[256,512]{1,0:T(8,128)(2,1)S(1)}, u32[]{:S(2)}, u32[]{:S(2)}) collective-permute-start(bf16[256,512]{1,0:T(8,128)(2,1)S(1)} %add_convert_fusion.7), channel_id=1, source_target_pairs={{0,2},{1,3},{2,0},{3,1},{4,6},{5,7},{6,4},{7,5},{8,10},{9,11},{10,... | collective-permute-start | bytes 786440 | tf_op jit(solution)/shard_map/ppermute | solution.py:574
  131.0 8.1 %collective-permute-start.19 = (f32[5,512]{1,0:T(8,128)S(1)}, f32[5,512]{1,0:T(8,128)S(1)}, u32[]{:S(2)}, u32[]{:S(2)}) collective-permute-start(f32[5,512]{1,0:T(8,128)S(1)} %add.217), channel_id=1, source_target_pairs={{0,16},{4,20},{8,24},{12,28},{16,0},{20,4},{24,8},{28,12},{1,17},{... | collective-permute-start | bytes 30728 | tf_op jit(solution)/shard_map/ppermute | solution.py:574
  139.1 8.8 %collective-permute-start.54 = (bf16[512,512]{1,0:T(8,128)(2,1)S(1)}, bf16[512,512]{1,0:T(8,128)(2,1)S(1)}, u32[]{:S(2)}, u32[]{:S(2)}) collective-permute-start(bf16[512,512]{1,0:T(8,128)(2,1)S(1)} %copy-done.29), channel_id=1, source_target_pairs={{0,1},{1,0},{2,3},{3,2},{4,5},{5,4},{6,7},{7,6},{8,9},{9,8},{10,11... | collective-permute-start | bytes 1572872 | tf_op jit(solution)/shard_map/ppermute | solution.py:574
  139.8 14.4 %collective-permute-start.21 = (bf16[1536,128]{1,0:T(8,128)(2,1)}, bf16[1536,128]{1,0:T(8,128)(2,1)S(1)}, u32[]{:S(2)}, u32[]{:S(2)}) collective-permute-start(bf16[1536,128]{1,0:T(8,128)(2,1)} %bitcast.94), channel_id=1, source_target_pairs={{0,1},{1,0},{2,3},{3,2},{4,5},{5,4},{6,7},{7,6},{8,9},{9,8},{10,11... | collective-permute-start | bytes 1179656 | tf_op jit(solution)/shard_map/ppermute | solution.py:574
  140.5 5.5 %collective-permute-start.34 = (bf16[128,512]{1,0:T(8,128)(2,1)S(1)}, bf16[128,512]{1,0:T(8,128)(2,1)S(1)}, u32[]{:S(2)}, u32[]{:S(2)}) collective-permute-start(bf16[128,512]{1,0:T(8,128)(2,1)S(1)} %constant_dynamic-slice_fusion.11), channel_id=1, source_target_pairs={{0,4},{4,0},{8,12},{12,8},{16,20},{20,16},{24,28},{28,24},{1,5},{5... | collective-permute-start | bytes 393224 | tf_op jit(solution)/shard_map/ppermute | solution.py:574
  146.0 4.6 %collective-permute-start.35 = (bf16[32,512]{1,0:T(8,128)(2,1)S(1)}, bf16[32,512]{1,0:T(8,128)(2,1)S(1)}, u32[]{:S(2)}, u32[]{:S(2)}) collective-permute-start(bf16[32,512]{1,0:T(8,128)(2,1)S(1)} %get-tuple-element.133), channel_id=1, source_target_pairs={{0,8},{4,12},{8,0},{12,4},{16,24},{20,28},{24,16},{28,20},{1,9},{5... | collective-permute-start | bytes 98312 | tf_op jit(solution)/shard_map/ppermute | solution.py:574
  147.6 5.1 %collective-permute-start.36 = (bf16[32,512]{1,0:T(8,128)(2,1)S(1)}, bf16[32,512]{1,0:T(8,128)(2,1)S(1)}, u32[]{:S(2)}, u32[]{:S(2)}) collective-permute-start(bf16[32,512]{1,0:T(8,128)(2,1)S(1)} %get-tuple-element.135), channel_id=1, source_target_pairs={{0,16},{4,20},{8,24},{12,28},{16,0},{20,4},{24,8},{28,12},{1,17},{... | collective-permute-start | bytes 98312 | tf_op jit(solution)/shard_map/ppermute | solution.py:574
  147.9 5.7 %collective-permute-start.37 = (bf16[32,512]{1,0:T(8,128)(2,1)S(1)}, bf16[32,512]{1,0:T(8,128)(2,1)S(1)}, u32[]{:S(2)}, u32[]{:S(2)}) collective-permute-start(bf16[32,512]{1,0:T(8,128)(2,1)S(1)} %get-tuple-element.134), channel_id=1, source_target_pairs={{0,24},{4,28},{8,16},{12,20},{16,8},{20,12},{24,0},{28,4},{1,25},{... | collective-permute-start | bytes 98312 | tf_op jit(solution)/shard_map/ppermute | solution.py:574
  150.6 38.0 %collective-permute-start.53 = (bf16[512,512]{1,0:T(8,128)(2,1)S(1)}, bf16[512,512]{1,0:T(8,128)(2,1)S(1)}, u32[]{:S(2)}, u32[]{:S(2)}) collective-permute-start(bf16[512,512]{1,0:T(8,128)(2,1)S(1)} %copy-done.27), channel_id=1, source_target_pairs={{0,1},{1,0},{2,3},{3,2},{4,5},{5,4},{6,7},{7,6},{8,9},{9,8},{10,11... | collective-permute-start | bytes 1572872 | tf_op jit(solution)/shard_map/ppermute | solution.py:574
  152.7 20.1 %collective-permute-start.20 = (bf16[1536,128]{1,0:T(8,128)(2,1)S(1)}, bf16[1536,128]{1,0:T(8,128)(2,1)S(1)}, u32[]{:S(2)}, u32[]{:S(2)}) collective-permute-start(bf16[1536,128]{1,0:T(8,128)(2,1)S(1)} %bitcast.93), channel_id=1, source_target_pairs={{0,1},{1,0},{2,3},{3,2},{4,5},{5,4},{6,7},{7,6},{8,9},{9,8},{10,11... | collective-permute-start | bytes 1179656 | tf_op jit(solution)/shard_map/ppermute | solution.py:574
  153.6 17.6 %collective-permute-start.44 = (bf16[512,512]{1,0:T(8,128)(2,1)S(1)}, bf16[512,512]{1,0:T(8,128)(2,1)S(1)}, u32[]{:S(2)}, u32[]{:S(2)}) collective-permute-start(bf16[512,512]{1,0:T(8,128)(2,1)S(1)} %add_convert_fusion.3), channel_id=1, source_target_pairs={{0,2},{1,3},{2,0},{3,1},{4,6},{5,7},{6,4},{7,5},{8,10},{9,11},{10,... | collective-permute-start | bytes 1572872 | tf_op jit(solution)/shard_map/ppermute | solution.py:574
  154.2 4.0 %collective-permute-start.38 = (bf16[32,512]{1,0:T(8,128)(2,1)S(1)}, bf16[32,512]{1,0:T(8,128)(2,1)S(1)}, u32[]{:S(2)}, u32[]{:S(2)}) collective-permute-start(bf16[32,512]{1,0:T(8,128)(2,1)S(1)} %get-tuple-element.121), channel_id=1, source_target_pairs={{0,8},{4,12},{8,0},{12,4},{16,24},{20,28},{24,16},{28,20},{1,9},{5... | collective-permute-start | bytes 98312 | tf_op jit(solution)/shard_map/ppermute | solution.py:574
  158.2 5.2 %collective-permute-start.39 = (bf16[32,512]{1,0:T(8,128)(2,1)S(1)}, bf16[32,512]{1,0:T(8,128)(2,1)S(1)}, u32[]{:S(2)}, u32[]{:S(2)}) collective-permute-start(bf16[32,512]{1,0:T(8,128)(2,1)S(1)} %get-tuple-element.121), channel_id=1, source_target_pairs={{0,16},{4,20},{8,24},{12,28},{16,0},{20,4},{24,8},{28,12},{1,17},{... | collective-permute-start | bytes 98312 | tf_op jit(solution)/shard_map/ppermute | solution.py:574
  163.4 5.7 %collective-permute-start.40 = (bf16[32,512]{1,0:T(8,128)(2,1)S(1)}, bf16[32,512]{1,0:T(8,128)(2,1)S(1)}, u32[]{:S(2)}, u32[]{:S(2)}) collective-permute-start(bf16[32,512]{1,0:T(8,128)(2,1)S(1)} %get-tuple-element.121), channel_id=1, source_target_pairs={{0,24},{4,28},{8,16},{12,20},{16,8},{20,12},{24,0},{28,4},{1,25},{... | collective-permute-start | bytes 98312 | tf_op jit(solution)/shard_map/ppermute | solution.py:574
  169.1 19.6 %collective-permute-start.55 = (bf16[512,512]{1,0:T(8,128)(2,1)S(1)}, bf16[512,512]{1,0:T(8,128)(2,1)S(1)}, u32[]{:S(2)}, u32[]{:S(2)}) collective-permute-start(bf16[512,512]{1,0:T(8,128)(2,1)S(1)} %add_convert_fusion.1), channel_id=1, source_target_pairs={{0,2},{1,3},{2,0},{3,1},{4,6},{5,7},{6,4},{7,5},{8,10},{9,11},{10,... | collective-permute-start | bytes 1572872 | tf_op jit(solution)/shard_map/ppermute | solution.py:574
  170.9 16.1 %collective-permute-start.22 = (bf16[1536,128]{1,0:T(8,128)(2,1)S(1)}, bf16[1536,128]{1,0:T(8,128)(2,1)S(1)}, u32[]{:S(2)}, u32[]{:S(2)}) collective-permute-start(bf16[1536,128]{1,0:T(8,128)(2,1)S(1)} %fusion), channel_id=1, source_target_pairs={{0,2},{1,3},{2,0},{3,1},{4,6},{5,7},{6,4},{7,5},{8,10},{9,11},{10,... | collective-permute-start | bytes 1179656 | tf_op jit(solution)/shard_map/ppermute | solution.py:574
  171.2 23.0 %collective-permute-start.41 = (bf16[128,512]{1,0:T(8,128)(2,1)S(1)}, bf16[128,512]{1,0:T(8,128)(2,1)S(1)}, u32[]{:S(2)}, u32[]{:S(2)}) collective-permute-start(bf16[128,512]{1,0:T(8,128)(2,1)S(1)} %bitcast.82), channel_id=1, source_target_pairs={{0,4},{4,0},{8,12},{12,8},{16,20},{20,16},{24,28},{28,24},{1,5},{5... | collective-permute-start | bytes 393224 | tf_op jit(solution)/shard_map/ppermute | solution.py:574
  172.9 32.9 %collective-permute-start.45 = (bf16[256,512]{1,0:T(8,128)(2,1)S(1)}, bf16[256,512]{1,0:T(8,128)(2,1)S(1)}, u32[]{:S(2)}, u32[]{:S(2)}) collective-permute-start(bf16[256,512]{1,0:T(8,128)(2,1)S(1)} %constant_dynamic-slice_fusion.7), channel_id=1, source_target_pairs={{0,4},{4,0},{8,12},{12,8},{16,20},{20,16},{24,28},{28,24},{1,5},{5... | collective-permute-start | bytes 786440 | tf_op jit(solution)/shard_map/ppermute | solution.py:574
  187.2 5.7 %collective-permute-start.23 = (bf16[768,128]{1,0:T(8,128)(2,1)S(1)}, bf16[768,128]{1,0:T(8,128)(2,1)S(1)}, u32[]{:S(2)}, u32[]{:S(2)}) collective-permute-start(bf16[768,128]{1,0:T(8,128)(2,1)S(1)} %constant_dynamic-slice_fusion.15), channel_id=1, source_target_pairs={{0,4},{4,0},{8,12},{12,8},{16,20},{20,16},{24,28},{28,24},{1,5},{5... | collective-permute-start | bytes 589832 | tf_op jit(solution)/shard_map/ppermute | solution.py:574
  188.9 16.9 %collective-permute-start.56 = (bf16[256,512]{1,0:T(8,128)(2,1)S(1)}, bf16[256,512]{1,0:T(8,128)(2,1)S(1)}, u32[]{:S(2)}, u32[]{:S(2)}) collective-permute-start(bf16[256,512]{1,0:T(8,128)(2,1)S(1)} %constant_dynamic-slice_fusion.3), channel_id=1, source_target_pairs={{0,4},{4,0},{8,12},{12,8},{16,20},{20,16},{24,28},{28,24},{1,5},{5... | collective-permute-start | bytes 786440 | tf_op jit(solution)/shard_map/ppermute | solution.py:574
  193.0 5.8 %collective-permute-start.24 = (bf16[192,128]{1,0:T(8,128)(2,1)S(1)}, bf16[192,128]{1,0:T(8,128)(2,1)S(1)}, u32[]{:S(2)}, u32[]{:S(2)}) collective-permute-start(bf16[192,128]{1,0:T(8,128)(2,1)S(1)} %get-tuple-element.130), channel_id=1, source_target_pairs={{0,8},{4,12},{8,0},{12,4},{16,24},{20,28},{24,16},{28,20},{1,9},{5... | collective-permute-start | bytes 147464 | tf_op jit(solution)/shard_map/ppermute | solution.py:574
  193.2 7.6 %collective-permute-start.25 = (bf16[192,128]{1,0:T(8,128)(2,1)S(1)}, bf16[192,128]{1,0:T(8,128)(2,1)S(1)}, u32[]{:S(2)}, u32[]{:S(2)}) collective-permute-start(bf16[192,128]{1,0:T(8,128)(2,1)S(1)} %get-tuple-element.132), channel_id=1, source_target_pairs={{0,16},{4,20},{8,24},{12,28},{16,0},{20,4},{24,8},{28,12},{1,17},{... | collective-permute-start | bytes 147464 | tf_op jit(solution)/shard_map/ppermute | solution.py:574
  194.2 6.7 %collective-permute-start.26 = (bf16[192,128]{1,0:T(8,128)(2,1)S(1)}, bf16[192,128]{1,0:T(8,128)(2,1)S(1)}, u32[]{:S(2)}, u32[]{:S(2)}) collective-permute-start(bf16[192,128]{1,0:T(8,128)(2,1)S(1)} %get-tuple-element.131), channel_id=1, source_target_pairs={{0,24},{4,28},{8,16},{12,20},{16,8},{20,12},{24,0},{28,4},{1,25},{... | collective-permute-start | bytes 147464 | tf_op jit(solution)/shard_map/ppermute | solution.py:574
  201.0 7.8 %collective-permute-start.27 = (bf16[192,128]{1,0:T(8,128)(2,1)S(1)}, bf16[192,128]{1,0:T(8,128)(2,1)S(1)}, u32[]{:S(2)}, u32[]{:S(2)}) collective-permute-start(bf16[192,128]{1,0:T(8,128)(2,1)S(1)} %get-tuple-element.123), channel_id=1, source_target_pairs={{0,8},{4,12},{8,0},{12,4},{16,24},{20,28},{24,16},{28,20},{1,9},{5... | collective-permute-start | bytes 147464 | tf_op jit(solution)/shard_map/ppermute | solution.py:574
  203.3 7.2 %collective-permute-start.28 = (bf16[192,128]{1,0:T(8,128)(2,1)S(1)}, bf16[192,128]{1,0:T(8,128)(2,1)S(1)}, u32[]{:S(2)}, u32[]{:S(2)}) collective-permute-start(bf16[192,128]{1,0:T(8,128)(2,1)S(1)} %get-tuple-element.123), channel_id=1, source_target_pairs={{0,16},{4,20},{8,24},{12,28},{16,0},{20,4},{24,8},{28,12},{1,17},{... | collective-permute-start | bytes 147464 | tf_op jit(solution)/shard_map/ppermute | solution.py:574
  204.1 6.6 %collective-permute-start.29 = (bf16[192,128]{1,0:T(8,128)(2,1)S(1)}, bf16[192,128]{1,0:T(8,128)(2,1)S(1)}, u32[]{:S(2)}, u32[]{:S(2)}) collective-permute-start(bf16[192,128]{1,0:T(8,128)(2,1)S(1)} %get-tuple-element.123), channel_id=1, source_target_pairs={{0,24},{4,28},{8,16},{12,20},{16,8},{20,12},{24,0},{28,4},{1,25},{... | collective-permute-start | bytes 147464 | tf_op jit(solution)/shard_map/ppermute | solution.py:574
  206.0 7.5 %collective-permute-start.57 = (bf16[64,512]{1,0:T(8,128)(2,1)S(1)}, bf16[64,512]{1,0:T(8,128)(2,1)S(1)}, u32[]{:S(2)}, u32[]{:S(2)}) collective-permute-start(bf16[64,512]{1,0:T(8,128)(2,1)S(1)} %get-tuple-element.124), channel_id=1, source_target_pairs={{0,8},{4,12},{8,0},{12,4},{16,24},{20,28},{24,16},{28,20},{1,9},{5... | collective-permute-start | bytes 196616 | tf_op jit(solution)/shard_map/ppermute | solution.py:574
  207.1 8.5 %collective-permute-start.58 = (bf16[64,512]{1,0:T(8,128)(2,1)S(1)}, bf16[64,512]{1,0:T(8,128)(2,1)S(1)}, u32[]{:S(2)}, u32[]{:S(2)}) collective-permute-start(bf16[64,512]{1,0:T(8,128)(2,1)S(1)} %get-tuple-element.126), channel_id=1, source_target_pairs={{0,16},{4,20},{8,24},{12,28},{16,0},{20,4},{24,8},{28,12},{1,17},{... | collective-permute-start | bytes 196616 | tf_op jit(solution)/shard_map/ppermute | solution.py:574
  208.8 8.4 %collective-permute-start.59 = (bf16[64,512]{1,0:T(8,128)(2,1)S(1)}, bf16[64,512]{1,0:T(8,128)(2,1)S(1)}, u32[]{:S(2)}, u32[]{:S(2)}) collective-permute-start(bf16[64,512]{1,0:T(8,128)(2,1)S(1)} %get-tuple-element.125), channel_id=1, source_target_pairs={{0,24},{4,28},{8,16},{12,20},{16,8},{20,12},{24,0},{28,4},{1,25},{... | collective-permute-start | bytes 196616 | tf_op jit(solution)/shard_map/ppermute | solution.py:574
  210.5 8.7 %collective-permute-start.46 = (bf16[64,512]{1,0:T(8,128)(2,1)S(1)}, bf16[64,512]{1,0:T(8,128)(2,1)S(1)}, u32[]{:S(2)}, u32[]{:S(2)}) collective-permute-start(bf16[64,512]{1,0:T(8,128)(2,1)S(1)} %get-tuple-element.127), channel_id=1, source_target_pairs={{0,8},{4,12},{8,0},{12,4},{16,24},{20,28},{24,16},{28,20},{1,9},{5... | collective-permute-start | bytes 196616 | tf_op jit(solution)/shard_map/ppermute | solution.py:574
  210.8 9.8 %collective-permute-start.47 = (bf16[64,512]{1,0:T(8,128)(2,1)S(1)}, bf16[64,512]{1,0:T(8,128)(2,1)S(1)}, u32[]{:S(2)}, u32[]{:S(2)}) collective-permute-start(bf16[64,512]{1,0:T(8,128)(2,1)S(1)} %get-tuple-element.129), channel_id=1, source_target_pairs={{0,16},{4,20},{8,24},{12,28},{16,0},{20,4},{24,8},{28,12},{1,17},{... | collective-permute-start | bytes 196616 | tf_op jit(solution)/shard_map/ppermute | solution.py:574
  213.4 8.9 %collective-permute-start.48 = (bf16[64,512]{1,0:T(8,128)(2,1)S(1)}, bf16[64,512]{1,0:T(8,128)(2,1)S(1)}, u32[]{:S(2)}, u32[]{:S(2)}) collective-permute-start(bf16[64,512]{1,0:T(8,128)(2,1)S(1)} %get-tuple-element.128), channel_id=1, source_target_pairs={{0,24},{4,28},{8,16},{12,20},{16,8},{20,12},{24,0},{28,4},{1,25},{... | collective-permute-start | bytes 196616 | tf_op jit(solution)/shard_map/ppermute | solution.py:574
  215.6 17.3 %collective-permute-start.30 = (bf16[768,128]{1,0:T(8,128)(2,1)S(1)}, bf16[768,128]{1,0:T(8,128)(2,1)S(1)}, u32[]{:S(2)}, u32[]{:S(2)}) collective-permute-start(bf16[768,128]{1,0:T(8,128)(2,1)S(1)} %bitcast.80), channel_id=1, source_target_pairs={{0,4},{4,0},{8,12},{12,8},{16,20},{20,16},{24,28},{28,24},{1,5},{5... | collective-permute-start | bytes 589832 | tf_op jit(solution)/shard_map/ppermute | solution.py:574
  217.3 5.6 %collective-permute-start.60 = (bf16[64,512]{1,0:T(8,128)(2,1)S(1)}, bf16[64,512]{1,0:T(8,128)(2,1)S(1)}, u32[]{:S(2)}, u32[]{:S(2)}) collective-permute-start(bf16[64,512]{1,0:T(8,128)(2,1)S(1)} %get-tuple-element.117), channel_id=1, source_target_pairs={{0,8},{4,12},{8,0},{12,4},{16,24},{20,28},{24,16},{28,20},{1,9},{5... | collective-permute-start | bytes 196616 | tf_op jit(solution)/shard_map/ppermute | solution.py:574
  219.2 5.9 %collective-permute-start.61 = (bf16[64,512]{1,0:T(8,128)(2,1)S(1)}, bf16[64,512]{1,0:T(8,128)(2,1)S(1)}, u32[]{:S(2)}, u32[]{:S(2)}) collective-permute-start(bf16[64,512]{1,0:T(8,128)(2,1)S(1)} %get-tuple-element.117), channel_id=1, source_target_pairs={{0,16},{4,20},{8,24},{12,28},{16,0},{20,4},{24,8},{28,12},{1,17},{... | collective-permute-start | bytes 196616 | tf_op jit(solution)/shard_map/ppermute | solution.py:574
  220.6 6.4 %collective-permute-start.62 = (bf16[64,512]{1,0:T(8,128)(2,1)S(1)}, bf16[64,512]{1,0:T(8,128)(2,1)S(1)}, u32[]{:S(2)}, u32[]{:S(2)}) collective-permute-start(bf16[64,512]{1,0:T(8,128)(2,1)S(1)} %get-tuple-element.117), channel_id=1, source_target_pairs={{0,24},{4,28},{8,16},{12,20},{16,8},{20,12},{24,0},{28,4},{1,25},{... | collective-permute-start | bytes 196616 | tf_op jit(solution)/shard_map/ppermute | solution.py:574
  222.4 5.9 %collective-permute-start.49 = (bf16[64,512]{1,0:T(8,128)(2,1)S(1)}, bf16[64,512]{1,0:T(8,128)(2,1)S(1)}, u32[]{:S(2)}, u32[]{:S(2)}) collective-permute-start(bf16[64,512]{1,0:T(8,128)(2,1)S(1)} %get-tuple-element.119), channel_id=1, source_target_pairs={{0,8},{4,12},{8,0},{12,4},{16,24},{20,28},{24,16},{28,20},{1,9},{5... | collective-permute-start | bytes 196616 | tf_op jit(solution)/shard_map/ppermute | solution.py:574
  222.9 5.5 %collective-permute-start.50 = (bf16[64,512]{1,0:T(8,128)(2,1)S(1)}, bf16[64,512]{1,0:T(8,128)(2,1)S(1)}, u32[]{:S(2)}, u32[]{:S(2)}) collective-permute-start(bf16[64,512]{1,0:T(8,128)(2,1)S(1)} %get-tuple-element.119), channel_id=1, source_target_pairs={{0,16},{4,20},{8,24},{12,28},{16,0},{20,4},{24,8},{28,12},{1,17},{... | collective-permute-start | bytes 196616 | tf_op jit(solution)/shard_map/ppermute | solution.py:574
  225.2 6.1 %collective-permute-start.51 = (bf16[64,512]{1,0:T(8,128)(2,1)S(1)}, bf16[64,512]{1,0:T(8,128)(2,1)S(1)}, u32[]{:S(2)}, u32[]{:S(2)}) collective-permute-start(bf16[64,512]{1,0:T(8,128)(2,1)S(1)} %get-tuple-element.119), channel_id=1, source_target_pairs={{0,24},{4,28},{8,16},{12,20},{16,8},{20,12},{24,0},{28,4},{1,25},{... | collective-permute-start | bytes 196616 | tf_op jit(solution)/shard_map/ppermute | solution.py:574
  227.0 6.8 %collective-permute-start.63 = (bf16[256,512]{1,0:T(8,128)(2,1)S(1)}, bf16[256,512]{1,0:T(8,128)(2,1)S(1)}, u32[]{:S(2)}, u32[]{:S(2)}) collective-permute-start(bf16[256,512]{1,0:T(8,128)(2,1)S(1)} %bitcast.78), channel_id=1, source_target_pairs={{0,4},{4,0},{8,12},{12,8},{16,20},{20,16},{24,28},{28,24},{1,5},{5... | collective-permute-start | bytes 786440 | tf_op jit(solution)/shard_map/ppermute | solution.py:574
  231.3 6.4 %collective-permute-start.52 = (bf16[256,512]{1,0:T(8,128)(2,1)S(1)}, bf16[256,512]{1,0:T(8,128)(2,1)S(1)}, u32[]{:S(2)}, u32[]{:S(2)}) collective-permute-start(bf16[256,512]{1,0:T(8,128)(2,1)S(1)} %bitcast.76), channel_id=1, source_target_pairs={{0,4},{4,0},{8,12},{12,8},{16,20},{20,16},{24,28},{28,24},{1,5},{5... | collective-permute-start | bytes 786440 | tf_op jit(solution)/shard_map/ppermute | solution.py:574
  (36 other events, 427.8 us)
